TPU v7x, 256 devices: a whole 4x4x8 slice. The times are simulated.
256 devices in a mesh: store: 64 (over x, z, core), head: 4 (over y).
Axes of the slice: x: 4, y: 4, z: 8, core: 2. Of those that a mesh axis runs over, the one named last changes fastest.
Arguments:
- queries: bfloat16 [16384, 8192], P('store', 'head'), may hold values from -1000 to 1000
- question_kv: bfloat16 [16384, 2048], P('store', 'head'), may hold values from -24 to 24
- pages: bfloat16 [1024, 96, 2048], P('store', 'head'), may hold values from -6 to 6
- page_scales: bfloat16 [1024, 96, 16], P('store', 'head'), may hold values from 0.29882812 to 3
- passage_ids: int32 [256, 4], P('store'), may hold values from 0 to 1023, as said below
Outputs:
- attended: bfloat16 [16384, 8192], P('store', 'head')
Inputs may be any that keep to these rules, and one draw needn't show every extreme that they name: `passage_ids`: among the 4 passages of each request of one aligned block of 4 requests, at most 2 lie on one store shard (the shard of id p is p // 16); in every block some shard holds exactly 2 of them.
All inputs are finite; a program needn't handle non-finite values.
Results may differ from a plain program's by a relative error of at most 0.0074.
Values may be sent and summed in bfloat16 or wider, within the bound.
A program may use at most 192 MiB of HBM per device.

v0:
```python
import jax
import jax.numpy as jnp
from jax import lax
from jax.sharding import PartitionSpec as P

QH = 64
KVH = 8
HD = 128
CAP = 2


rope_theta = 500000.0


def rotate_keys(keys, offsets):
    half_dim = keys.shape[-1] // 2
    freqs = jnp.exp(
        jnp.arange(half_dim, dtype=jnp.float32)
        * (-2.0 * jnp.log(jnp.float32(rope_theta)) / keys.shape[-1])
    )
    angles = offsets[:, None] * freqs[None, :]
    cosine = jnp.cos(angles)[:, None, None, :]
    sine = jnp.sin(angles)[:, None, None, :]
    first = keys[..., :half_dim]
    second = keys[..., half_dim:]
    return jnp.concatenate(
        [first * cosine - second * sine, second * cosine + first * sine], axis=-1
    )


def attend(query_rows, key_rows, value_rows):
    qlen = query_rows.shape[1]
    total = key_rows.shape[1]
    scores = jnp.einsum(
        "bqkgd,bskd->bkgqs", query_rows, key_rows, preferred_element_type=jnp.float32
    ) / jnp.sqrt(jnp.float32(query_rows.shape[-1]))
    key_pos = jnp.arange(total)
    query_pos = jnp.arange(qlen) + (total - qlen)
    allowed = key_pos[None, :] <= query_pos[:, None]
    scores = jnp.where(allowed, scores, -jnp.inf)
    highest = jnp.max(scores, axis=-1, keepdims=True)
    raised = jnp.exp(scores - highest)
    probs = (raised / jnp.sum(raised, axis=-1, keepdims=True)).astype(jnp.bfloat16)
    result = jnp.einsum("bkgqs,bskd->bqkgd", probs, value_rows, preferred_element_type=jnp.float32)
    return result.astype(jnp.bfloat16)


def per_device(queries, question_kv, pages, page_scales, passage_ids):
    shards = lax.axis_size("store")
    groups_axis = lax.axis_size("head")
    requests, per_request = passage_ids.shape
    fetches = requests * per_request
    stored, part_tokens, lanes = pages.shape
    passage_len = part_tokens * groups_axis
    kv_local = KVH // groups_axis
    groups = QH // KVH
    head_dim = HD
    question_len = queries.shape[0] // requests
    flat_ids = passage_ids.reshape(fetches)
    shard_of = flat_ids // stored
    within = flat_ids % stored
    counter = jnp.arange(fetches)
    same_shard = shard_of[:, None] == shard_of[None, :]
    earlier = counter[None, :] < counter[:, None]
    order_rank = jnp.sum(same_shard & earlier, axis=1)
    slot_index = shard_of * CAP + order_rank
    matches = slot_index[:, None] == jnp.arange(shards * CAP)[None, :]
    wanted_table = jnp.sum(jnp.where(matches, within[:, None], 0), axis=0).reshape(shards, CAP)
    asked = lax.all_to_all(wanted_table, "store", split_axis=0, concat_axis=0, tiled=True)
    asked_flat = asked.reshape(shards * CAP)
    send_pages = jnp.take(pages, asked_flat, axis=0).reshape(shards, CAP, part_tokens, lanes)
    send_scales = jnp.take(page_scales, asked_flat, axis=0).reshape(
        shards, CAP, part_tokens, 2 * KVH
    )
    got_pages, got_scales = (
        lax.all_to_all(
            lax.all_to_all(send_pages, "store", split_axis=0, concat_axis=0, tiled=True),
            "head",
            split_axis=3,
            concat_axis=2,
            tiled=True,
        ),
        lax.all_to_all(
            lax.all_to_all(send_scales, "store", split_axis=0, concat_axis=0, tiled=True),
            "head",
            split_axis=3,
            concat_axis=2,
            tiled=True,
        ),
    )
    mine_pages = jnp.take(
        got_pages.reshape(shards * CAP, passage_len, 2 * kv_local * head_dim), slot_index, axis=0
    )
    mine_scales = jnp.take(
        got_scales.reshape(shards * CAP, passage_len, 2 * kv_local), slot_index, axis=0
    )
    mine_pages = mine_pages.reshape(requests, per_request, passage_len, kv_local, 2, head_dim)
    mine_scales = mine_scales.reshape(requests, per_request, passage_len, kv_local, 2)
    plain = mine_pages.astype(jnp.float32) * mine_scales.astype(jnp.float32)[..., None]
    offsets = jnp.arange(per_request, dtype=jnp.float32) * passage_len
    key_part = (
        rotate_keys(plain[..., 0, :], offsets)
        .astype(jnp.bfloat16)
        .reshape(requests, per_request * passage_len, kv_local, head_dim)
    )
    value_part = (
        plain[..., 1, :]
        .astype(jnp.bfloat16)
        .reshape(requests, per_request * passage_len, kv_local, head_dim)
    )
    question_rows = question_kv.reshape(requests, question_len, kv_local, 2, head_dim)
    key_rows = jnp.concatenate([key_part, question_rows[:, :, :, 0, :]], axis=1)
    value_rows = jnp.concatenate([value_part, question_rows[:, :, :, 1, :]], axis=1)
    query_rows = queries.reshape(requests, question_len, kv_local, groups, head_dim)
    block_reqs = 1
    for candidate in range(1, requests + 1):
        if requests % candidate == 0 and candidate * question_len <= max(512, question_len):
            block_reqs = candidate
    block_count = requests // block_reqs

    def one_block(items):
        return attend(items[0], items[1], items[2])

    result = lax.map(
        one_block,
        (
            query_rows.reshape((block_count, block_reqs) + query_rows.shape[1:]),
            key_rows.reshape((block_count, block_reqs) + key_rows.shape[1:]),
            value_rows.reshape((block_count, block_reqs) + value_rows.shape[1:]),
        ),
    )
    return result.reshape(requests * question_len, kv_local * groups * head_dim)


def solution(mesh):
    return jax.shard_map(
        per_device,
        mesh=mesh,
        in_specs=(
            P("store", "head"),
            P("store", "head"),
            P("store", "head", None),
            P("store", "head", None),
            P("store", None),
        ),
        out_specs=P("store", "head"),
        check_vma=False,
    )
```

profile of v0, /device:TPU:1, one launch (start us, length us, event | category | flops | bytes accessed | tf_op | source)
XLA Modules:
  0.0 673.8 jit_solution(2987581753842102248)
XLA Ops:
  0.0 0.9 reshape.333
  0.9 0.2 convert_reduce_fusion
  1.2 0.1 all_to_all.34
  1.3 22.1 %all_to_all.49 = s32[64,1,2]{2,1,0:T(1,128)S(1)} all-to-all(s32[64,1,2]{2,1,0:T(1,128)S(1)} %bitcast.80), channel_id=1, replica_groups=mesh['store'=64,'head'=4] {'store'}, dimensions={0} | all-to-all | bytes 1024 | tf_op jit(solution)/shard_map/all_to_all | solution.py:69
  23.4 0.5 broadcast.386
  23.9 0.7 reduce.3
  24.6 0.1 reshape.335
  25.0 7.9 %gather_fusion = bf16[128,24,2048]{2,1,0:T(8,128)(2,1)} fusion(bf16[16,24,2048]{2,1,0:T(8,128)(2,1)S(1)} %copy-done, s32[1024]{0:T(1024)S(1)} %pad_clamp_fusion.1), kind=kCustom, calls=%fused_computation | custom fusion | bytes 25166336 | tf_op jit(solution)/shard_map/jit(_take)/gather | solution.py:71
  32.9 0.7 gather_fusion.2
  33.6 0.2 fusion.29
  33.9 1.3 reshape.387
  35.2 4.7 all-to-all-start.3
  39.9 10.8 %broadcast_select_fusion = bf16[64,2,24,2048]{3,2,1,0:T(8,128)(2,1)} fusion(bf16[64,2,24,2048]{3,2,1,0:T(8,128)(2,1)} %bitcast.67, pred[64,2]{1,0:T(8,128)(4,1)S(1)} %copy.93), kind=kLoop, calls=%fused_computation.5 | loop fusion | flops 6291456 | bytes 25165952 | tf_op jit(solution)/shard_map/jit(_take)/select_n | solution.py:71
  50.7 10.6 %all-to-all-start.1 = ((bf16[64,2,24,2048]{3,2,1,0:T(8,128)(2,1)}), bf16[64,2,24,2048]{3,2,1,0:T(8,128)(2,1)}, u32[]{:S(2)}, u32[]{:S(2)}) async-start(bf16[64,2,24,2048]{3,2,1,0:T(8,128)(2,1)} %broadcast_select_fusion), calls=%async_computation.1 | async-start | bytes 25165824 | tf_op jit(solution)/shard_map/all_to_all | solution.py:77
  61.3 0.7 reshape.388
  62.0 0.6 copy.98
  62.6 0.8 reshape.389
  63.4 273.5 %all-to-all-done.1 = bf16[64,2,24,2048]{3,2,1,0:T(8,128)(2,1)} async-done(((bf16[64,2,24,2048]{3,2,1,0:T(8,128)(2,1)}), bf16[64,2,24,2048]{3,2,1,0:T(8,128)(2,1)}, u32[]{:S(2)}, u32[]{:S(2)}) %all-to-all-start.1) | async-done | bytes 12582944 | tf_op jit(solution)/shard_map/all_to_all | solution.py:77
  337.0 4.2 all-to-all-start.4
  341.1 39.1 %copy.94 = bf16[64,2,24,2048]{0,2,1,3:T(8,128)(2,1)} copy(bf16[64,2,24,2048]{3,2,1,0:T(8,128)(2,1)} %all-to-all-done.1) | data formatting | bytes 25165824 | tf_op jit(solution)/shard_map/all_to_all | solution.py:77
  380.3 37.3 %reshape.385 = bf16[4,2,786432]{2,1,0:T(2,128)(2,1)} reshape(bf16[2048,2,24,64]{3,2,1,0:T(8,128)(2,1)} %bitcast.65) | data formatting | bytes 25165824
  417.6 6.8 %all-to-all-start.2 = ((bf16[4,2,786432]{2,1,0:T(2,128)(2,1)}), bf16[4,2,786432]{2,1,0:T(2,128)(2,1)}, u32[]{:S(2)}, u32[]{:S(2)}) async-start(bf16[4,2,786432]{2,1,0:T(2,128)(2,1)} %reshape.385), calls=%async_computation.2 | async-start | bytes 25165824 | tf_op jit(solution)/shard_map/all_to_all | solution.py:76
  424.5 1.2 copy.119
  426.1 0.4 fusion.27
  426.5 0.2 reshape.390
  426.7 0.8 copy.115
  427.5 0.3 reshape.375
  427.8 0.6 gather_fusion.3
  428.5 1.0 copy.103
  429.5 133.8 %all-to-all-done.2 = bf16[4,2,786432]{2,1,0:T(2,128)(2,1)} async-done(((bf16[4,2,786432]{2,1,0:T(2,128)(2,1)}), bf16[4,2,786432]{2,1,0:T(2,128)(2,1)}, u32[]{:S(2)}, u32[]{:S(2)}) %all-to-all-start.2) | async-done | bytes 12582944 | tf_op jit(solution)/shard_map/all_to_all | solution.py:76
  563.2 36.6 %reshape.386 = bf16[2048,2,24,64]{3,2,1,0:T(8,128)(2,1)} reshape(bf16[4,2,786432]{2,1,0:T(2,128)(2,1)} %all-to-all-done.2) | data formatting | bytes 25165824
  599.9 33.1 %copy.113 = bf16[64,2,24,4,512]{4,3,2,1,0:T(4,128)(2,1)} copy(bf16[64,2,24,4,512]{0,2,1,4,3:T(8,128)(2,1)} %bitcast.66) | data formatting | bytes 25165824 | tf_op jit(solution)/shard_map/all_to_all | solution.py:76
  633.0 13.0 %copy.96 = bf16[64,2,4,24,512]{4,3,2,1,0:T(8,128)(2,1)} copy(bf16[64,2,4,24,512]{4,2,3,1,0:T(4,128)(2,1)} %bitcast.68) | data formatting | bytes 25165824 | tf_op jit(solution)/shard_map/all_to_all | solution.py:76
  645.9 6.4 gather_fusion.1
  652.4 2.4 gather.27
  654.7 3.9 convert_multiply_fusion
  658.6 1.1 slice.35
  659.7 1.7 slice.44
  661.5 2.5 subtract_convert_fusion
  664.0 0.1 copy.107
  664.1 0.1 copy.106
  664.3 0.2 copy.104
  664.4 0.8 copy-done.3
  665.2 1.3 fusion.8
  666.6 3.6 fusion.28
  670.2 1.6 fusion.7
  671.8 0.7 copy.110
  672.5 1.3 reshape.340
  (37 shorter events, 1.0 us)
Async XLA Ops:
  0.0 25.0 %copy-start = (bf16[16,24,2048]{2,1,0:T(8,128)(2,1)S(1)}, bf16[16,24,2048]{2,1,0:T(8,128)(2,1)}, u32[]{:S(2)}) copy-start(bf16[16,24,2048]{2,1,0:T(8,128)(2,1)} %param.7) | copy-start | bytes 4718596
  25.0 7.9 %copy-start.2 = (bf16[16,24,16]{1,2,0:T(8,128)(2,1)S(1)}, bf16[16,24,16]{1,2,0:T(8,128)(2,1)}, u32[]{:S(2)}) copy-start(bf16[16,24,16]{1,2,0:T(8,128)(2,1)} %param.8) | copy-start | bytes 36868
  35.2 15.5 %all-to-all-start.3 = ((bf16[64,2,384]{2,1,0:T(2,128)(2,1)}), bf16[64,2,384]{2,1,0:T(2,128)(2,1)S(1)}, u32[]{:S(2)}, u32[]{:S(2)}) async-start(bf16[64,2,384]{2,1,0:T(2,128)(2,1)} %reshape.387), calls=%async_computation.3 | async-start | bytes 196608 | tf_op jit(solution)/shard_map/all_to_all | solution.py:84
  50.7 286.3 %all-to-all-start.1 = ((bf16[64,2,24,2048]{3,2,1,0:T(8,128)(2,1)}), bf16[64,2,24,2048]{3,2,1,0:T(8,128)(2,1)}, u32[]{:S(2)}, u32[]{:S(2)}) async-start(bf16[64,2,24,2048]{3,2,1,0:T(8,128)(2,1)} %broadcast_select_fusion), calls=%async_computation.1 | async-start | bytes 25165824 | tf_op jit(solution)/shard_map/all_to_all | solution.py:77
  337.0 80.6 %all-to-all-start.4 = ((bf16[4,2,6144]{2,1,0:T(2,128)(2,1)}), bf16[4,2,6144]{2,1,0:T(2,128)(2,1)S(1)}, u32[]{:S(2)}, u32[]{:S(2)}) async-start(bf16[4,2,6144]{2,1,0:T(2,128)(2,1)} %reshape.389), calls=%async_computation.4 | async-start | bytes 196608 | tf_op jit(solution)/shard_map/all_to_all | solution.py:83
  417.6 6.8 %copy-start.6 = (s32[4,4]{1,0:T(4,128)S(1)}, s32[4,4]{1,0:T(4,128)}, u32[]{:S(2)}) copy-start(s32[4,4]{1,0:T(4,128)} %param.9) | copy-start | bytes 196
  417.6 7.0 %copy-start.4 = (bf16[256,2048]{1,0:T(8,128)(2,1)S(1)}, bf16[256,2048]{1,0:T(8,128)(2,1)}, u32[]{:S(2)}) copy-start(bf16[256,2048]{1,0:T(8,128)(2,1)} %param.5) | copy-start | bytes 3145732
  417.6 8.2 %copy-start.5 = (bf16[256,512]{1,0:T(8,128)(2,1)S(1)}, bf16[256,512]{1,0:T(8,128)(2,1)}, u32[]{:S(2)}) copy-start(bf16[256,512]{1,0:T(8,128)(2,1)} %param.6) | copy-start | bytes 786436
  417.6 145.7 %all-to-all-start.2 = ((bf16[4,2,786432]{2,1,0:T(2,128)(2,1)}), bf16[4,2,786432]{2,1,0:T(2,128)(2,1)}, u32[]{:S(2)}, u32[]{:S(2)}) async-start(bf16[4,2,786432]{2,1,0:T(2,128)(2,1)} %reshape.385), calls=%async_computation.2 | async-start | bytes 25165824 | tf_op jit(solution)/shard_map/all_to_all | solution.py:76
  664.0 1.2 copy-start.3
  670.2 3.6 copy-start.1
where the time goes:
time: 676 us; the launch traced here: 674 us
  waiting for transfers between devices  407 us (60%)
  local copies, waits for them, and re-layouts  192 us (28%)
  starting transfers between devices  26.3 us (4%)
  other arithmetic  22.4 us (3%)
  blocking collectives  22.1 us (3%)
    all_to_all x1, waiting for transfers between devices, per_device(): lax.all_to_all(send_pages, 'store', split_axis=0, concat_axis=0, tiled=True)  274 us
    all_to_all x1, waiting for transfers between devices, per_device(): lax.all_to_all(lax.all_to_all(send_pages, 'store', split_axis=0, concat_a...  134 us
    unnamed x21, local copies, waits for them, and re-layouts  79 us
    all_to_all x2, local copies, waits for them, and re-layouts, per_device(): lax.all_to_all(lax.all_to_all(send_pages, 'store', split_axis=0, concat_a...  46.1 us
    all_to_all x1, local copies, waits for them, and re-layouts, per_device(): lax.all_to_all(send_pages, 'store', split_axis=0, concat_axis=0, tiled=True)  39.1 us
    all_to_all x1, blocking collectives, per_device(): lax.all_to_all(wanted_table, 'store', split_axis=0, concat_axis=0, tiled=...  22.1 us
  transfers between devices with their start and end apart: 4, of which 2 were waited for; matrix products, arithmetic and copies ran while one was open for 14% of the time, Pallas kernels for 0%

commit v1 on v0

--- a/solution.py
+++ b/solution.py
@@ -1,13 +1,34 @@
+import math
+
+import numpy as np
 import jax
 import jax.numpy as jnp
 from jax import lax
+from jax.experimental import pallas as pl
+from jax.experimental.pallas import tpu as pltpu
 from jax.sharding import PartitionSpec as P
 
 QH = 64
 KVH = 8
 HD = 128
+NPAS = 4
+PLEN = 96
 CAP = 2
-
+QLEN = 64
+R_DEV = 4
+P_DEV = 16
+XS, ZS, CORES, HEADS = 4, 8, 2, 4
+SHARDS = XS * CORES
+TOK = PLEN // HEADS
+ROWS = 2 * TOK
+LANES = 2 * HD
+SLOTS = 4
+FETCH = R_DEV * NPAS
+GROUPS = QH // KVH
+PART = 4 * HD
+PKEYS = NPAS * PLEN
+KEYS = PKEYS + QLEN
+MESH = pl.DeviceIdType.MESH
 
 rope_theta = 500000.0
 
@@ -45,7 +66,7 @@
     return result.astype(jnp.bfloat16)
 
 
-def per_device(queries, question_kv, pages, page_scales, passage_ids):
+def general(queries, question_kv, pages, page_scales, passage_ids):
     shards = lax.axis_size("store")
     groups_axis = lax.axis_size("head")
     requests, per_request = passage_ids.shape
@@ -112,24 +133,355 @@
     key_rows = jnp.concatenate([key_part, question_rows[:, :, :, 0, :]], axis=1)
     value_rows = jnp.concatenate([value_part, question_rows[:, :, :, 1, :]], axis=1)
     query_rows = queries.reshape(requests, question_len, kv_local, groups, head_dim)
-    block_reqs = 1
-    for candidate in range(1, requests + 1):
-        if requests % candidate == 0 and candidate * question_len <= max(512, question_len):
-            block_reqs = candidate
-    block_count = requests // block_reqs
 
     def one_block(items):
         return attend(items[0], items[1], items[2])
 
     result = lax.map(
-        one_block,
-        (
-            query_rows.reshape((block_count, block_reqs) + query_rows.shape[1:]),
-            key_rows.reshape((block_count, block_reqs) + key_rows.shape[1:]),
-            value_rows.reshape((block_count, block_reqs) + value_rows.shape[1:]),
+        one_block, (query_rows[:, None], key_rows[:, None], value_rows[:, None])
+    )
+    return result.reshape(requests * question_len, kv_local * groups * head_dim)
+
+
+def rope_tables():
+    half = HD // 2
+    freqs = np.exp(
+        np.arange(half, dtype=np.float32)
+        * np.float32(-2.0 * np.log(np.float32(rope_theta)) / np.float32(HD))
+    ).astype(np.float32)
+    angles = (np.arange(NPAS, dtype=np.float32) * np.float32(PLEN))[:, None] * freqs[None, :]
+    angles = angles.astype(np.float64)
+    cosine = np.concatenate([np.cos(angles), np.cos(angles)], axis=1)
+    sine = np.concatenate([-np.sin(angles), np.sin(angles)], axis=1)
+    spread = lambda table: np.repeat(table[:, None, :], 8, axis=1).astype(np.float32)
+    return spread(cosine), spread(sine)
+
+
+def kernel(
+    ids_ref, pages_ref, scales_ref, q_ref, qkv_ref, cos_ref, sin_ref,
+    out_ref, flag_ref,
+    ysend, g0, g1, g2, g3, s0, s1, s2, s3, l0, l1, l2, l3,
+    idv, ids, want, mine, kv,
+    y_send, y_recv, x_send, x_recv, z_send, z_recv, i_send, i_recv, local_sem,
+):
+    gathered, outgoing, landed = (g0, g1, g2, g3), (s0, s1, s2, s3), (l0, l1, l2, l3)
+    store, head = lax.axis_index("store"), lax.axis_index("head")
+    x, z, core = store // (ZS * CORES), (store // CORES) % ZS, store % CORES
+    turn = 1 - 2 * core
+
+    def at(x_, z_, core_):
+        return ((x_ + 2 * XS) % XS * ZS + z_ % ZS) * CORES + core_
+
+    def spot(x_, core_):
+        return (x_ + 2 * XS) % XS * CORES + core_
+
+    barrier = pltpu.get_barrier_semaphore()
+    peers = [(store, (head + c) % HEADS) for c in range(1, HEADS)]
+    peers += [(at(x + 1, z, core), head), (at(x - 1, z, core), head), (at(x, z, 1 - core), head)]
+    peers += [(at(x, z + d, core), head) for d in range(1, ZS)]
+    for peer in peers:
+        pl.semaphore_signal(barrier, inc=1, device_id=peer, device_id_type=MESH)
+
+    planes, over = [], 0
+    for i in range(FETCH):
+        one = ids_ref[i // NPAS, i % NPAS]
+        plane = (one // P_DEV // CORES) % ZS
+        rank = 0
+        for other in planes:
+            rank = rank + jnp.where(other == plane, 1, 0)
+        planes.append(plane)
+        over = jnp.maximum(over, rank)
+        mine[i] = plane * SLOTS + jnp.minimum(rank, SLOTS - 1)
+    lane8 = lax.broadcasted_iota(jnp.int32, (8, 128), 1)
+    tile = jnp.where(lane8 == FETCH, over, 0)
+    for i in range(FETCH):
+        tile = jnp.where(lane8 == i, ids_ref[i // NPAS, i % NPAS], tile)
+    idv[z] = tile
+
+    lane = lax.broadcasted_iota(jnp.int32, (TOK, 128), 1)
+    for hh in range(HEADS):
+
+        def one_page(p, held, hh=hh):
+            scale = scales_ref[p].astype(jnp.float32)
+            halves, kept = [], []
+            for g in range(2):
+                col = 2 * (2 * hh + g)
+                codes = pages_ref[p, :, PART * hh + LANES * g : PART * hh + LANES * (g + 1)]
+                codes = codes.astype(jnp.float32)
+                value = codes[:, HD:] * scale[:, col + 1 : col + 2]
+                halves.append(jnp.concatenate([codes[:, :HD], value], axis=1))
+                kept.append(jnp.where(lane == p, scale[:, col : col + 1], held[g]))
+            ysend[hh, p] = jnp.concatenate(halves, axis=0).astype(jnp.bfloat16)
+            return tuple(kept)
+
+        none = jnp.zeros((TOK, 128), jnp.float32)
+        kept = lax.fori_loop(0, P_DEV, one_page, (none, none))
+        ysend[hh, P_DEV, :, :HD] = jnp.concatenate(kept, axis=0).astype(jnp.bfloat16)
+        ysend[hh, P_DEV, :, HD:] = jnp.zeros((ROWS, HD), jnp.bfloat16)
+
+    pl.semaphore_wait(barrier, len(peers))
+
+    def id_copy(step):
+        return pltpu.make_async_remote_copy(
+            src_ref=idv.at[z], dst_ref=idv.at[z],
+            send_sem=i_send.at[step], recv_sem=i_recv.at[step],
+            device_id=(at(x, z + step, core), head), device_id_type=MESH,
+        )
+
+    def y_copy(c):
+        to = (head + HEADS - c) % HEADS
+        return pltpu.make_async_remote_copy(
+            src_ref=ysend.at[to], dst_ref=gathered[c].at[spot(x, core)],
+            send_sem=y_send.at[c], recv_sem=y_recv.at[c],
+            device_id=(store, to), device_id_type=MESH,
+        )
+
+    def x_copy(c, kind):
+        slot, to = (
+            (spot(x, core), at(x + 1, z, core)),
+            (spot(x, core), at(x - 1, z, core)),
+            (spot(x - turn, core), at(x + turn, z, core)),
+            (spot(x, core), at(x, z, 1 - core)),
+            (spot(x - 1, core), at(x, z, 1 - core)),
+            (spot(x + 1, core), at(x, z, 1 - core)),
+            (spot(x + 2, core), at(x, z, 1 - core)),
+        )[kind]
+        return pltpu.make_async_remote_copy(
+            src_ref=gathered[c].at[slot], dst_ref=gathered[c].at[slot],
+            send_sem=x_send.at[c, kind], recv_sem=x_recv.at[c, kind],
+            device_id=(to, head), device_id_type=MESH,
+        )
+
+    def z_copy(c, step):
+        return pltpu.make_async_remote_copy(
+            src_ref=outgoing[c].at[step], dst_ref=landed[c].at[z],
+            send_sem=z_send.at[c, step], recv_sem=z_recv.at[c, step],
+            device_id=(at(x, z + step, core), head), device_id_type=MESH,
+        )
+
+    def x_start(c):
+        if c > 0:
+            y_copy(c).wait_recv()
+        if c == HEADS - 1:
+            g3[spot(x, core), P_DEV, :, HD:] = jnp.broadcast_to(flag, (ROWS, HD)).astype(
+                jnp.bfloat16
+            )
+        for kind in (0, 1, 3):
+            x_copy(c, kind).start()
+
+    def x_forward(c):
+        x_copy(c, 0).wait_recv()
+        x_copy(c, 1).wait_recv()
+        for kind in (2, 4, 5):
+            x_copy(c, kind).start()
+
+    def x_last(c):
+        x_copy(c, 2).wait_recv()
+        x_copy(c, 6).start()
+
+    def x_done(c):
+        for kind in (3, 4, 5, 6):
+            x_copy(c, kind).wait_recv()
+
+    rows_lane = lax.broadcasted_iota(jnp.int32, (ROWS, 128), 1)
+
+    def finished(c, code):
+        page = code % P_DEV
+        shard = (code // P_DEV) % (XS * ZS * CORES)
+        k = code // (XS * ZS * CORES * P_DEV)
+        place = (shard // (ZS * CORES)) * CORES + shard % CORES
+        block = gathered[c][place, page]
+        scales = gathered[c][place, P_DEV, :, :HD].astype(jnp.float32)
+        scale = jnp.sum(jnp.where(rows_lane == page, scales, 0.0), axis=1, keepdims=True)
+        key = block[:, :HD].astype(jnp.float32) * scale
+        turned = key * cos_ref[k, 0:1] + pltpu.roll(key, HD // 2, 1) * sin_ref[k, 0:1]
+        return turned.astype(jnp.bfloat16), block[:, HD:]
+
+    def z_start(c):
+        def one_dest(i, carry):
+            step = (i * 3) % ZS
+            to = (z + step) % ZS
+            for j in range(SLOTS):
+                key, value = finished(c, want[to * SLOTS + j])
+                outgoing[c][step, j, :, :HD] = key
+                outgoing[c][step, j, :, HD:] = value
+            z_copy(c, step).start()
+            return carry
+
+        lax.fori_loop(1, ZS, one_dest, 0)
+        for j in range(SLOTS):
+            key, value = finished(c, want[z * SLOTS + j])
+            landed[c][z, j, :, :HD] = key
+            landed[c][z, j, :, HD:] = value
+
+    for step in range(1, ZS):
+        id_copy(step).start()
+    for c in range(1, HEADS):
+        y_copy(c).start()
+    own = pltpu.make_async_copy(ysend.at[head], g0.at[spot(x, core)], local_sem)
+    own.start()
+    own.wait()
+    x_start(0)
+
+    for step in range(1, ZS):
+        id_copy(step).wait_recv()
+    to_smem = pltpu.make_async_copy(idv, ids, local_sem)
+    to_smem.start()
+    to_smem.wait()
+
+    def scan(dest, worst):
+        count = 0
+        chosen = [0] * SLOTS
+        for i in range(FETCH):
+            one = ids[dest, 0, i]
+            hit = (one // P_DEV // CORES) % ZS == z
+            for j in range(SLOTS):
+                chosen[j] = jnp.where(
+                    hit & (count == j), one + (i % NPAS) * (XS * ZS * CORES * P_DEV), chosen[j]
+                )
+            count = count + jnp.where(hit, 1, 0)
+        for j in range(SLOTS):
+            want[dest * SLOTS + j] = chosen[j]
+        return jnp.maximum(worst, ids[dest, 0, FETCH])
+
+    worst = lax.fori_loop(0, ZS, scan, jnp.int32(0))
+    flag = jnp.where(worst >= SLOTS, 1.0, 0.0)
+
+    x_start(1)
+    x_forward(0)
+    x_last(0)
+    x_start(2)
+    x_done(0)
+    z_start(0)
+    x_forward(1)
+    x_last(1)
+    x_start(3)
+    x_done(1)
+    z_start(1)
+    x_forward(2)
+    x_last(2)
+    x_done(2)
+    z_start(2)
+    x_forward(3)
+    x_last(3)
+    x_done(3)
+    z_start(3)
+
+    flags = g3[0, P_DEV, :, HD:].astype(jnp.float32)
+    for place in range(1, SHARDS):
+        flags = jnp.maximum(flags, g3[place, P_DEV, :, HD:].astype(jnp.float32))
+    flag_ref[...] = flags[:8]
+
+    def arrived(c):
+        def one(step, carry):
+            z_copy(c, step).wait_recv()
+            return carry
+
+        lax.fori_loop(1, ZS, one, 0)
+
+    for c in range(HEADS):
+        arrived(c)
+
+    col = lax.broadcasted_iota(jnp.int32, (GROUPS * QLEN, QLEN), 1)
+    row = lax.broadcasted_iota(jnp.int32, (GROUPS * QLEN, QLEN), 0) % QLEN
+    seen = col <= row
+
+    def one_request(r, carry):
+        rows = pl.ds(pl.multiple_of(r * QLEN, QLEN), QLEN)
+        for c in range(HEADS):
+            blocks = []
+            for k in range(NPAS):
+                spot_ = mine[r * NPAS + k]
+                blocks.append(landed[c][spot_ // SLOTS, spot_ % SLOTS].astype(jnp.float32))
+            for g in range(2):
+                part = jnp.concatenate([b[g * TOK : (g + 1) * TOK] for b in blocks], axis=0)
+                kv[g, c * PLEN : (c + 1) * PLEN, :] = part.astype(jnp.bfloat16)
+        for g in range(2):
+            kv[g, PKEYS:, :] = qkv_ref[rows, g * LANES : (g + 1) * LANES]
+            query = jnp.concatenate(
+                [
+                    q_ref[rows, (g * GROUPS + j) * HD : (g * GROUPS + j + 1) * HD]
+                    for j in range(GROUPS)
+                ],
+                axis=0,
+            )
+            dims = (((1,), (1,)), ((), ()))
+            scale = jnp.float32(1.0 / math.sqrt(HD))
+            past = scale * lax.dot_general(
+                query, kv[g, :PKEYS, :HD], dims, preferred_element_type=jnp.float32
+            )
+            now = scale * lax.dot_general(
+                query, kv[g, PKEYS:, :HD], dims, preferred_element_type=jnp.float32
+            )
+            now = jnp.where(seen, now, -jnp.inf)
+            top = jnp.maximum(
+                jnp.max(past, axis=1, keepdims=True), jnp.max(now, axis=1, keepdims=True)
+            )
+            past = jnp.exp(past - top)
+            now = jnp.exp(now - top)
+            total = jnp.sum(past, axis=1, keepdims=True) + jnp.sum(now, axis=1, keepdims=True)
+            inverse = 1.0 / total
+            past = (past * inverse).astype(jnp.bfloat16)
+            now = (now * inverse).astype(jnp.bfloat16)
+            result = jnp.dot(past, kv[g, :PKEYS, HD:], preferred_element_type=jnp.float32)
+            result = result + jnp.dot(now, kv[g, PKEYS:, HD:], preferred_element_type=jnp.float32)
+            for j in range(GROUPS):
+                out_ref[rows, (g * GROUPS + j) * HD : (g * GROUPS + j + 1) * HD] = result[
+                    j * QLEN : (j + 1) * QLEN
+                ].astype(jnp.bfloat16)
+        return carry
+
+    lax.fori_loop(0, R_DEV, one_request, 0)
+
+    for step in range(1, ZS):
+        id_copy(step).wait_send()
+    for c in range(1, HEADS):
+        y_copy(c).wait_send()
+    for c in range(HEADS):
+        for kind in range(7):
+            x_copy(c, kind).wait_send()
+        for step in range(1, ZS):
+            z_copy(c, step).wait_send()
+
+
+def fast(queries, question_kv, pages, page_scales, passage_ids):
+    cosine, sine = rope_tables()
+    vmem = pl.BlockSpec(memory_space=pltpu.VMEM)
+    block = (ROWS, LANES)
+    dma = pltpu.SemaphoreType.DMA
+    return pl.pallas_call(
+        kernel,
+        out_shape=(
+            jax.ShapeDtypeStruct(queries.shape, jnp.bfloat16),
+            jax.ShapeDtypeStruct((8, 128), jnp.float32),
         ),
-    )
-    return result.reshape(requests * question_len, kv_local * groups * head_dim)
+        in_specs=[pl.BlockSpec(memory_space=pltpu.SMEM)] + [vmem] * 6,
+        out_specs=(vmem, vmem),
+        scratch_shapes=[pltpu.VMEM((HEADS, P_DEV + 1) + block, jnp.bfloat16)]
+        + [pltpu.VMEM((SHARDS, P_DEV + 1) + block, jnp.bfloat16)] * HEADS
+        + [pltpu.VMEM((ZS, SLOTS) + block, jnp.bfloat16)] * (2 * HEADS)
+        + [
+            pltpu.VMEM((ZS, 8, 128), jnp.int32),
+            pltpu.SMEM((ZS, 8, 128), jnp.int32),
+            pltpu.SMEM((ZS * SLOTS,), jnp.int32),
+            pltpu.SMEM((FETCH,), jnp.int32),
+            pltpu.VMEM((2, KEYS, LANES), jnp.bfloat16),
+            dma((HEADS,)), dma((HEADS,)),
+            dma((HEADS, 7)), dma((HEADS, 7)),
+            dma((HEADS, ZS)), dma((HEADS, ZS)),
+            dma((ZS,)), dma((ZS,)),
+            dma,
+        ],
+        compiler_params=pltpu.CompilerParams(
+            collective_id=0, has_side_effects=True, vmem_limit_bytes=48 * 1024 * 1024
+        ),
+    )(passage_ids, pages, page_scales, queries, question_kv, jnp.asarray(cosine), jnp.asarray(sine))
+
+
+def per_device(queries, question_kv, pages, page_scales, passage_ids):
+    args = (queries, question_kv, pages, page_scales, passage_ids)
+    result, flags = fast(*args)
+    return lax.cond(flags[0, 0] > 0, lambda: general(*args), lambda: result)
 
 
 def solution(mesh):

time: 676 us -> 126 us (0.19)
  waiting for transfers between devices: 407 us -> 0 us
  local copies, waits for them, and re-layouts: 192 us -> 5.28 us
  Pallas kernels: 0 us -> 120 us
  starting transfers between devices: 26.3 us -> 0 us
  other arithmetic: 22.4 us -> 0 us
  blocking collectives: 22.1 us -> 0 us
    all_to_all x4 -> x0, waiting for transfers between devices: 407 us -> none  [the longest x1 274 us: per_device(): lax.all_to_all(send_pages, 'store', split_axis=0, concat_axis=0, tiled=True)]
    pallas_call x0 -> x1, Pallas kernels: none -> 120 us  [fast(): pl.pallas_call(kernel, out_shape=(jax.ShapeDtypeStruct(queries.shape, jnp...]
    all_to_all x7 -> x0, local copies, waits for them, and re-layouts: 86.5 us -> none  [the longest x2 46.1 us: per_device(): lax.all_to_all(lax.all_to_all(send_pages, 'store', split_axis=0, concat_a...]
    unnamed x21 -> x16, local copies, waits for them, and re-layouts: 79 us -> 4.76 us
    all_to_all x4 -> x0, starting transfers between devices: 26.3 us -> none  [the longest x1 10.6 us: per_device(): lax.all_to_all(send_pages, 'store', split_axis=0, concat_axis=0, tiled=True)]
    all_to_all x1 -> x0, blocking collectives: 22.1 us -> none  [per_device(): lax.all_to_all(wanted_table, 'store', split_axis=0, concat_axis=0, tiled=...]
    gather x6 -> x0, local copies, waits for them, and re-layouts: 18 us -> none  [the longest x2 8.77 us: per_device(): jnp.take(got_pages.reshape(shards * CAP, passage_len, 2 * kv_local * head...]
    select_n x4 -> x0, other arithmetic: 10.8 us -> none  [the longest x2 10.8 us: per_device(): jnp.take(pages, asked_flat, axis=0).reshape(shards, CAP, part_tokens, lanes)]
  transfers between devices with their start and end apart: 4 -> 0, of which waited for: 2 -> 0; matrix products, arithmetic and copies ran while one was open for 14% -> 0% of each run, Pallas kernels for 0% -> 0%
where the time goes in v1:
time: 126 us
  Pallas kernels  120 us (95%)
  local copies, waits for them, and re-layouts  5.28 us (4%)
    pallas_call x1, Pallas kernels, fast(): pl.pallas_call(kernel, out_shape=(jax.ShapeDtypeStruct(queries.shape, jnp...  120 us
    unnamed x16, local copies, waits for them, and re-layouts  4.76 us

profile of v1, /device:TPU:1, one launch (start us, length us, event | category | flops | bytes accessed | tf_op | source)
XLA Modules:
  0.0 126.1 jit_solution(9551147029494907409)
XLA Ops:
  0.0 0.0 copy-start.7
  0.0 0.0 copy-start.3
  0.0 1.0 copy.126.scales_ref
  1.0 0.0 copy-start
  1.0 0.7 copy-done
  1.7 0.0 copy-start.1
  1.7 0.7 copy-done.1
  2.5 0.0 copy-start.2
  2.5 0.0 copy-start.4
  2.5 0.0 copy-start.5
  2.5 119.8 %shard_map.75 = (bf16[256,2048]{1,0:T(8,128)(2,1)}, f32[8,128]{1,0:T(8,128)S(1)}) custom-call(s32[4,4]{1,0:T(4,128)} %ids_ref.1, bf16[16,24,2048]{2,1,0:T(8,128)(2,1)} %pages_ref.1, bf16[16,24,16]{2,1,0:T(8,128)(2,1)S(1)} %copy.126.scales_ref, bf16[256,2048]{1,0:T(8,128)(2,1)} %q_ref.1, bf16[256,512]{1,0:T(8,128)(2,1)} %qkv_ref.1, f32[4,8,128]{2,1,0:T(8,128)S(1)} %copy-done, ...), custom_call_target="tpu_custom_call" | custom-call | tf_op jit(solution)/shard_map/pallas_call | solution.py:452
  122.3 0.5 slice.22
  123.5 0.0 copy-done.7
  123.5 0.0 copy-done.3
  123.5 0.0 copy-done.2
  123.5 0.0 copy-done.4
  123.5 0.0 copy-done.5
  123.5 0.2 conditional.1
  123.7 2.3 %copy.160 = bf16[256,2048]{1,0:T(8,128)(2,1)} copy(bf16[256,2048]{1,0:T(8,128)(2,1)} %get-tuple-element.55) | data formatting | bytes 2097152
Async XLA Ops:
  0.0 123.5 %copy-start.7 = (s32[4,4]{1,0:T(4,128)S(1)}, s32[4,4]{1,0:T(4,128)}, u32[]{:S(2)}) copy-start(s32[4,4]{1,0:T(4,128)} %ids_ref.1) | copy-start | bytes 196
  0.0 123.5 %copy-start.3 = (bf16[16,24,16]{1,2,0:T(8,128)(2,1)S(1)}, bf16[16,24,16]{1,2,0:T(8,128)(2,1)}, u32[]{:S(2)}) copy-start(bf16[16,24,16]{1,2,0:T(8,128)(2,1)} %param.14) | copy-start | bytes 36868
  1.0 0.7 copy-start
  1.7 0.7 copy-start.1
  2.5 121.0 %copy-start.2 = (bf16[16,24,2048]{2,1,0:T(8,128)(2,1)S(1)}, bf16[16,24,2048]{2,1,0:T(8,128)(2,1)}, u32[]{:S(2)}) copy-start(bf16[16,24,2048]{2,1,0:T(8,128)(2,1)} %pages_ref.1) | copy-start | bytes 4718596
  2.5 121.0 %copy-start.4 = (bf16[256,2048]{1,0:T(8,128)(2,1)S(1)}, bf16[256,2048]{1,0:T(8,128)(2,1)}, u32[]{:S(2)}) copy-start(bf16[256,2048]{1,0:T(8,128)(2,1)} %q_ref.1) | copy-start | bytes 3145732
  2.5 121.0 %copy-start.5 = (bf16[256,512]{1,0:T(8,128)(2,1)S(1)}, bf16[256,512]{1,0:T(8,128)(2,1)}, u32[]{:S(2)}) copy-start(bf16[256,512]{1,0:T(8,128)(2,1)} %qkv_ref.1) | copy-start | bytes 786436

commit v2 on v1

v2 whole, which is shorter than its diff:
```python
import math

import numpy as np
import jax
import jax.numpy as jnp
from jax import lax
from jax.experimental import pallas as pl
from jax.experimental.pallas import tpu as pltpu
from jax.sharding import PartitionSpec as P

QH = 64
KVH = 8
HD = 128
NPAS = 4
PLEN = 96
CAP = 2
QLEN = 64
R_DEV = 4
P_DEV = 16
XS, ZS, CORES, HEADS = 4, 8, 2, 4
SHARDS = XS * CORES
TOK = PLEN // HEADS
ROWS = 2 * TOK
LANES = 2 * HD
SLOTS = 4
FETCH = R_DEV * NPAS
GROUPS = QH // KVH
PART = 4 * HD
PIECE = NPAS * TOK
PKEYS = NPAS * PLEN
KEYS = PKEYS + QLEN
CHUNKS = 2 * HEADS
MESH = pl.DeviceIdType.MESH

rope_theta = 500000.0


def rotate_keys(keys, offsets):
    half_dim = keys.shape[-1] // 2
    freqs = jnp.exp(
        jnp.arange(half_dim, dtype=jnp.float32)
        * (-2.0 * jnp.log(jnp.float32(rope_theta)) / keys.shape[-1])
    )
    angles = offsets[:, None] * freqs[None, :]
    cosine = jnp.cos(angles)[:, None, None, :]
    sine = jnp.sin(angles)[:, None, None, :]
    first = keys[..., :half_dim]
    second = keys[..., half_dim:]
    return jnp.concatenate(
        [first * cosine - second * sine, second * cosine + first * sine], axis=-1
    )


def attend(query_rows, key_rows, value_rows):
    qlen = query_rows.shape[1]
    total = key_rows.shape[1]
    scores = jnp.einsum(
        "bqkgd,bskd->bkgqs", query_rows, key_rows, preferred_element_type=jnp.float32
    ) / jnp.sqrt(jnp.float32(query_rows.shape[-1]))
    key_pos = jnp.arange(total)
    query_pos = jnp.arange(qlen) + (total - qlen)
    allowed = key_pos[None, :] <= query_pos[:, None]
    scores = jnp.where(allowed, scores, -jnp.inf)
    highest = jnp.max(scores, axis=-1, keepdims=True)
    raised = jnp.exp(scores - highest)
    probs = (raised / jnp.sum(raised, axis=-1, keepdims=True)).astype(jnp.bfloat16)
    result = jnp.einsum("bkgqs,bskd->bqkgd", probs, value_rows, preferred_element_type=jnp.float32)
    return result.astype(jnp.bfloat16)


def general(queries, question_kv, pages, page_scales, passage_ids):
    shards = lax.axis_size("store")
    groups_axis = lax.axis_size("head")
    requests, per_request = passage_ids.shape
    fetches = requests * per_request
    stored, part_tokens, lanes = pages.shape
    passage_len = part_tokens * groups_axis
    kv_local = KVH // groups_axis
    groups = QH // KVH
    head_dim = HD
    question_len = queries.shape[0] // requests
    flat_ids = passage_ids.reshape(fetches)
    shard_of = flat_ids // stored
    within = flat_ids % stored
    counter = jnp.arange(fetches)
    same_shard = shard_of[:, None] == shard_of[None, :]
    earlier = counter[None, :] < counter[:, None]
    order_rank = jnp.sum(same_shard & earlier, axis=1)
    slot_index = shard_of * CAP + order_rank
    matches = slot_index[:, None] == jnp.arange(shards * CAP)[None, :]
    wanted_table = jnp.sum(jnp.where(matches, within[:, None], 0), axis=0).reshape(shards, CAP)
    asked = lax.all_to_all(wanted_table, "store", split_axis=0, concat_axis=0, tiled=True)
    asked_flat = asked.reshape(shards * CAP)
    send_pages = jnp.take(pages, asked_flat, axis=0).reshape(shards, CAP, part_tokens, lanes)
    send_scales = jnp.take(page_scales, asked_flat, axis=0).reshape(
        shards, CAP, part_tokens, 2 * KVH
    )
    got_pages, got_scales = (
        lax.all_to_all(
            lax.all_to_all(send_pages, "store", split_axis=0, concat_axis=0, tiled=True),
            "head",
            split_axis=3,
            concat_axis=2,
            tiled=True,
        ),
        lax.all_to_all(
            lax.all_to_all(send_scales, "store", split_axis=0, concat_axis=0, tiled=True),
            "head",
            split_axis=3,
            concat_axis=2,
            tiled=True,
        ),
    )
    mine_pages = jnp.take(
        got_pages.reshape(shards * CAP, passage_len, 2 * kv_local * head_dim), slot_index, axis=0
    )
    mine_scales = jnp.take(
        got_scales.reshape(shards * CAP, passage_len, 2 * kv_local), slot_index, axis=0
    )
    mine_pages = mine_pages.reshape(requests, per_request, passage_len, kv_local, 2, head_dim)
    mine_scales = mine_scales.reshape(requests, per_request, passage_len, kv_local, 2)
    plain = mine_pages.astype(jnp.float32) * mine_scales.astype(jnp.float32)[..., None]
    offsets = jnp.arange(per_request, dtype=jnp.float32) * passage_len
    key_part = (
        rotate_keys(plain[..., 0, :], offsets)
        .astype(jnp.bfloat16)
        .reshape(requests, per_request * passage_len, kv_local, head_dim)
    )
    value_part = (
        plain[..., 1, :]
        .astype(jnp.bfloat16)
        .reshape(requests, per_request * passage_len, kv_local, head_dim)
    )
    question_rows = question_kv.reshape(requests, question_len, kv_local, 2, head_dim)
    key_rows = jnp.concatenate([key_part, question_rows[:, :, :, 0, :]], axis=1)
    value_rows = jnp.concatenate([value_part, question_rows[:, :, :, 1, :]], axis=1)
    query_rows = queries.reshape(requests, question_len, kv_local, groups, head_dim)

    def one_block(items):
        return attend(items[0], items[1], items[2])

    result = lax.map(
        one_block, (query_rows[:, None], key_rows[:, None], value_rows[:, None])
    )
    return result.reshape(requests * question_len, kv_local * groups * head_dim)


def rope_table():
    half = HD // 2
    freqs = np.exp(
        np.arange(half, dtype=np.float32)
        * np.float32(-2.0 * np.log(np.float32(rope_theta)) / np.float32(HD))
    ).astype(np.float32)
    angles = (np.arange(NPAS, dtype=np.float32) * np.float32(PLEN))[:, None] * freqs[None, :]
    angles = angles.astype(np.float64)
    cosine = np.concatenate([np.cos(angles), np.cos(angles)], axis=1)
    sine = np.concatenate([-np.sin(angles), np.sin(angles)], axis=1)
    return np.stack([cosine, sine] * 4, axis=1).astype(np.float32)


def kernel(
    ids_ref, pages_ref, scales_ref, q_ref, qkv_ref, rope_ref,
    out_ref, flag_ref,
    p0, p1, p2, p3, yk1, yk2, yk3, yv1, yv2, yv3, gk0, gk1, gk2, gk3, gv0, gv1, gv2, gv3,
    s0, s1, s2, s3, s4, s5, s6, s7, l0, l1, l2, l3, l4, l5, l6, l7,
    idv, ids, want, mine, rope, queries, question, keys, values, probs, result,
    y_send, y_recv, x_send, x_recv, z_send, z_recv, i_send, i_recv, in_sem, out_sem,
):
    parts = (p0, p1, p2, p3)
    outward = (None, yk1, yk2, yk3, None, yv1, yv2, yv3)
    gathered = (gk0, gk1, gk2, gk3, gv0, gv1, gv2, gv3)
    outgoing = (s0, s1, s2, s3, s4, s5, s6, s7)
    landed = (l0, l1, l2, l3, l4, l5, l6, l7)
    store, head = lax.axis_index("store"), lax.axis_index("head")
    x, z, core = store // (ZS * CORES), (store // CORES) % ZS, store % CORES
    turn = 1 - 2 * core

    def at(x_, z_, core_):
        return ((x_ + 2 * XS) % XS * ZS + z_ % ZS) * CORES + core_

    def spot(x_, core_):
        return (x_ + 2 * XS) % XS * CORES + core_

    here = spot(x, core)

    barrier = pltpu.get_barrier_semaphore()
    peers = [(store, (head + c) % HEADS) for c in range(1, HEADS)]
    peers += [(at(x + 1, z, core), head), (at(x - 1, z, core), head), (at(x, z, 1 - core), head)]
    peers += [(at(x, z + d, core), head) for d in range(1, ZS)]
    for peer in peers:
        pl.semaphore_signal(barrier, inc=1, device_id=peer, device_id_type=MESH)

    def page_copy(c):
        to = (head + HEADS - c) % HEADS
        lanes = pl.ds(pl.multiple_of(to * PART, PART), PART)
        return pltpu.make_async_copy(pages_ref.at[:, lanes], parts[c], in_sem.at[c])

    for c in range(HEADS):
        page_copy(c).start()
    rope_copy = pltpu.make_async_copy(rope_ref, rope, in_sem.at[HEADS])
    query_copy = pltpu.make_async_copy(q_ref, queries, in_sem.at[HEADS + 1])
    question_copy = pltpu.make_async_copy(qkv_ref, question, in_sem.at[HEADS + 2])
    rope_copy.start()
    query_copy.start()
    question_copy.start()

    planes, over = [], 0
    for i in range(FETCH):
        one = ids_ref[i // NPAS, i % NPAS]
        plane = (one // P_DEV // CORES) % ZS
        rank = 0
        for other in planes:
            rank = rank + jnp.where(other == plane, 1, 0)
        planes.append(plane)
        over = jnp.maximum(over, rank)
        mine[i] = plane * SLOTS + jnp.minimum(rank, SLOTS - 1)
    lane8 = lax.broadcasted_iota(jnp.int32, (8, 128), 1)
    tile = jnp.where(lane8 == FETCH, over, 0)
    for i in range(FETCH):
        tile = jnp.where(lane8 == i, ids_ref[i // NPAS, i % NPAS], tile)
    idv[z] = tile

    def id_copy(step):
        return pltpu.make_async_remote_copy(
            src_ref=idv.at[z], dst_ref=idv.at[z],
            send_sem=i_send.at[step], recv_sem=i_recv.at[step],
            device_id=(at(x, z + step, core), head), device_id_type=MESH,
        )

    def y_copy(n):
        c = n % HEADS
        to = (head + HEADS - c) % HEADS
        return pltpu.make_async_remote_copy(
            src_ref=outward[n], dst_ref=gathered[n].at[here],
            send_sem=y_send.at[n], recv_sem=y_recv.at[n],
            device_id=(store, to), device_id_type=MESH,
        )

    def x_copy(n, kind):
        slot, to = (
            (here, at(x + 1, z, core)),
            (here, at(x - 1, z, core)),
            (spot(x - turn, core), at(x + turn, z, core)),
            (here, at(x, z, 1 - core)),
            (spot(x - 1, core), at(x, z, 1 - core)),
            (spot(x + 1, core), at(x, z, 1 - core)),
            (spot(x + 2, core), at(x, z, 1 - core)),
        )[kind]
        return pltpu.make_async_remote_copy(
            src_ref=gathered[n].at[slot], dst_ref=gathered[n].at[slot],
            send_sem=x_send.at[n, kind], recv_sem=x_recv.at[n, kind],
            device_id=(to, head), device_id_type=MESH,
        )

    def z_copy(n, step):
        return pltpu.make_async_remote_copy(
            src_ref=outgoing[n].at[step], dst_ref=landed[n].at[z],
            send_sem=z_send.at[n, step], recv_sem=z_recv.at[n, step],
            device_id=(at(x, z + step, core), head), device_id_type=MESH,
        )

    lane = lax.broadcasted_iota(jnp.int32, (TOK, 128), 1)
    pick_row = lax.broadcasted_iota(jnp.int32, (P_DEV * 2 * KVH, 128), 0)
    pick_lane = lax.broadcasted_iota(jnp.int32, (P_DEV * 2 * KVH, 128), 1)

    def scales_of(col):
        pick = jnp.where(pick_row == 2 * KVH * pick_lane + col, 1.0, 0.0).astype(jnp.bfloat16)
        return lax.dot_general(
            scales_ref[...], pick, (((0,), (0,)), ((), ())), preferred_element_type=jnp.float32
        )

    def lay_out(c, key_blocks, value_blocks, *at_):
        first = 4 * ((head + HEADS - c) % HEADS)
        scales = [scales_of(first + j) for j in range(4)]
        key_blocks[(*at_, P_DEV)] = jnp.concatenate([scales[0], scales[2]], axis=0).astype(jnp.bfloat16)

        def two_pages(i, carry):
            pair = pl.ds(pl.multiple_of(i * ROWS, ROWS), ROWS)
            codes = [
                parts[c][pair, LANES * g : LANES * (g + 1)].astype(jnp.float32) for g in range(2)
            ]
            for half in range(2):
                p, rows = 2 * i + half, slice(half * TOK, (half + 1) * TOK)
                value_half = []
                for g in range(2):
                    scale = jnp.sum(
                        jnp.where(lane == p, scales[2 * g + 1], 0.0), axis=1, keepdims=True
                    )
                    value_half.append(codes[g][rows, HD:] * scale)
                key_half = [codes[g][rows, :HD] for g in range(2)]
                key_blocks[(*at_, p)] = jnp.concatenate(key_half, axis=0).astype(jnp.bfloat16)
                value_blocks[(*at_, p)] = jnp.concatenate(value_half, axis=0).astype(jnp.bfloat16)
            return carry

        lax.fori_loop(0, P_DEV // 2, two_pages, 0)

    def x_start(n):
        if n % HEADS > 0:
            y_copy(n).wait_recv()
        if n == HEADS - 1:
            gk3[here, P_DEV, :, HD // 2 :] = jnp.broadcast_to(flag, (ROWS, HD // 2)).astype(
                jnp.bfloat16
            )
        for kind in (0, 1, 3):
            x_copy(n, kind).start()

    def x_forward(n):
        x_copy(n, 0).wait_recv()
        x_copy(n, 1).wait_recv()
        for kind in (2, 4, 5):
            x_copy(n, kind).start()

    def x_last(n):
        x_copy(n, 2).wait_recv()
        x_copy(n, 6).start()

    def x_done(n):
        for kind in (3, 4, 5, 6):
            x_copy(n, kind).wait_recv()

    rows_lane = lax.broadcasted_iota(jnp.int32, (ROWS, 128), 1)

    def finished(n, code):
        slot = code % P_DEV
        shard = (code // P_DEV) % (XS * ZS * CORES)
        k = code // (XS * ZS * CORES * P_DEV)
        place = (shard // (ZS * CORES)) * CORES + shard % CORES
        block = gathered[n][place, slot]
        if n >= HEADS:
            return block
        scales = gathered[n][place, P_DEV].astype(jnp.float32)
        scale = jnp.sum(jnp.where(rows_lane == slot, scales, 0.0), axis=1, keepdims=True)
        key = block.astype(jnp.float32) * scale
        turned = key * rope[k, 0:1] + pltpu.roll(key, HD // 2, 1) * rope[k, 1:2]
        return turned.astype(jnp.bfloat16)

    def z_start(n):
        def one_dest(i, carry):
            step = (i * 3) % ZS
            to = (z + step) % ZS
            for j in range(SLOTS):
                outgoing[n][step, j] = finished(n, want[to * SLOTS + j])
            z_copy(n, step).start()
            return carry

        lax.fori_loop(1, ZS, one_dest, 0)
        for j in range(SLOTS):
            landed[n][z, j] = finished(n, want[z * SLOTS + j])

    page_copy(0).wait()
    lay_out(0, gk0, gv0, here)
    pl.semaphore_wait(barrier, len(peers))
    for step in range(1, ZS):
        id_copy(step).start()
    x_start(0)
    for c in range(1, HEADS):
        page_copy(c).wait()
        lay_out(c, outward[c], outward[HEADS + c])
        y_copy(c).start()
    for c in range(1, HEADS):
        y_copy(HEADS + c).start()
    rope_copy.wait()

    for step in range(1, ZS):
        id_copy(step).wait_recv()
    to_smem = pltpu.make_async_copy(idv, ids, in_sem.at[HEADS + 3])
    to_smem.start()
    to_smem.wait()

    def scan(dest, worst):
        count = 0
        chosen = [0] * SLOTS
        for i in range(FETCH):
            one = ids[dest, 0, i]
            hit = (one // P_DEV // CORES) % ZS == z
            for j in range(SLOTS):
                chosen[j] = jnp.where(
                    hit & (count == j), one + (i % NPAS) * (XS * ZS * CORES * P_DEV), chosen[j]
                )
            count = count + jnp.where(hit, 1, 0)
        for j in range(SLOTS):
            want[dest * SLOTS + j] = chosen[j]
        return jnp.maximum(worst, ids[dest, 0, FETCH])

    x_forward(0)
    worst = lax.fori_loop(0, ZS, scan, jnp.int32(0))
    flag = jnp.where(worst >= SLOTS, 1.0, 0.0)

    for n in range(CHUNKS):
        if n > 0:
            x_forward(n)
        if n + 1 < CHUNKS:
            x_start(n + 1)
        x_last(n)
        x_done(n)
        z_start(n)

    flags = gk3[0, P_DEV].astype(jnp.float32)
    for place in range(1, SHARDS):
        flags = jnp.maximum(flags, gk3[place, P_DEV].astype(jnp.float32))
    flag_ref[...] = flags[:8]

    def arrived(n):
        def one(step, carry):
            z_copy(n, step).wait_recv()
            return carry

        lax.fori_loop(1, ZS, one, 0)

    def passages(n, r):
        blocks = []
        for k in range(NPAS):
            place = mine[r * NPAS + k]
            blocks.append(landed[n][place // SLOTS, place % SLOTS].astype(jnp.float32))
        return [
            jnp.concatenate([b[g * TOK : (g + 1) * TOK] for b in blocks], axis=0).astype(
                jnp.bfloat16
            )
            for g in range(2)
        ]

    for c in range(HEADS):
        arrived(c)
    query_copy.wait()
    question_copy.wait()

    col = lax.broadcasted_iota(jnp.int32, (GROUPS * QLEN, QLEN), 1)
    row = lax.broadcasted_iota(jnp.int32, (GROUPS * QLEN, QLEN), 0) % QLEN
    seen = col <= row

    def weigh(r, carry):
        rows = pl.ds(pl.multiple_of(r * QLEN, QLEN), QLEN)
        for c in range(HEADS):
            for g, part in enumerate(passages(c, r)):
                keys[g, c * PIECE : (c + 1) * PIECE, :] = part
        for g in range(2):
            keys[g, PKEYS:, :] = question[rows, g * LANES : g * LANES + HD]
            values[r, g, PKEYS:, :] = question[rows, g * LANES + HD : (g + 1) * LANES]
            query = jnp.concatenate(
                [
                    queries[rows, (g * GROUPS + j) * HD : (g * GROUPS + j + 1) * HD]
                    for j in range(GROUPS)
                ],
                axis=0,
            )
            dims = (((1,), (1,)), ((), ()))
            scale = jnp.float32(1.0 / math.sqrt(HD))
            past = scale * lax.dot_general(
                query, keys[g, :PKEYS, :], dims, preferred_element_type=jnp.float32
            )
            now = scale * lax.dot_general(
                query, keys[g, PKEYS:, :], dims, preferred_element_type=jnp.float32
            )
            now = jnp.where(seen, now, -jnp.inf)
            top = jnp.maximum(
                jnp.max(past, axis=1, keepdims=True), jnp.max(now, axis=1, keepdims=True)
            )
            past = jnp.exp(past - top)
            now = jnp.exp(now - top)
            total = jnp.sum(past, axis=1, keepdims=True) + jnp.sum(now, axis=1, keepdims=True)
            inverse = 1.0 / total
            probs[r, g, :, :PKEYS] = (past * inverse).astype(jnp.bfloat16)
            probs[r, g, :, PKEYS:] = (now * inverse).astype(jnp.bfloat16)
        return carry

    lax.fori_loop(0, R_DEV, weigh, 0)

    for c in range(HEADS):
        arrived(HEADS + c)

        def place_values(r, carry, c=c):
            for g, part in enumerate(passages(HEADS + c, r)):
                values[r, g, c * PIECE : (c + 1) * PIECE, :] = part
            return carry

        lax.fori_loop(0, R_DEV, place_values, 0)

    def out_copy(r):
        rows = pl.ds(pl.multiple_of(r * QLEN, QLEN), QLEN)
        return pltpu.make_async_copy(result.at[r], out_ref.at[rows], out_sem.at[r])

    def mix(r, carry):
        for g in range(2):
            mixed = jnp.dot(probs[r, g], values[r, g], preferred_element_type=jnp.float32)
            for j in range(GROUPS):
                result[r, :, (g * GROUPS + j) * HD : (g * GROUPS + j + 1) * HD] = mixed[
                    j * QLEN : (j + 1) * QLEN
                ].astype(jnp.bfloat16)
        out_copy(r).start()
        return carry

    lax.fori_loop(0, R_DEV, mix, 0)

    for step in range(1, ZS):
        id_copy(step).wait_send()
    for n in range(CHUNKS):
        if n % HEADS > 0:
            y_copy(n).wait_send()
        for kind in range(7):
            x_copy(n, kind).wait_send()
        for step in range(1, ZS):
            z_copy(n, step).wait_send()
    for r in range(R_DEV):
        out_copy(r).wait()


def fast(queries, question_kv, pages, page_scales, passage_ids):
    vmem = pl.BlockSpec(memory_space=pltpu.VMEM)
    hbm = pl.BlockSpec(memory_space=pl.ANY)
    block = (ROWS, HD)
    dma, bf16 = pltpu.SemaphoreType.DMA, jnp.bfloat16
    rows = pages.reshape(P_DEV * TOK, 2 * KVH * HD)
    scales = page_scales.transpose(0, 2, 1).reshape(P_DEV * 2 * KVH, TOK)
    return pl.pallas_call(
        kernel,
        out_shape=(
            jax.ShapeDtypeStruct(queries.shape, bf16),
            jax.ShapeDtypeStruct((8, 128), jnp.float32),
        ),
        in_specs=[pl.BlockSpec(memory_space=pltpu.SMEM), hbm, vmem, hbm, hbm, hbm],
        out_specs=(hbm, vmem),
        scratch_shapes=[pltpu.VMEM((P_DEV * TOK, PART), bf16)] * HEADS
        + [pltpu.VMEM((P_DEV + 1,) + block, bf16)] * (HEADS - 1)
        + [pltpu.VMEM((P_DEV,) + block, bf16)] * (HEADS - 1)
        + [pltpu.VMEM((SHARDS, P_DEV + 1) + block, bf16)] * HEADS
        + [pltpu.VMEM((SHARDS, P_DEV) + block, bf16)] * HEADS
        + [pltpu.VMEM((ZS, SLOTS) + block, bf16)] * (2 * CHUNKS)
        + [
            pltpu.VMEM((ZS, 8, 128), jnp.int32),
            pltpu.SMEM((ZS, 8, 128), jnp.int32),
            pltpu.SMEM((ZS * SLOTS,), jnp.int32),
            pltpu.SMEM((FETCH,), jnp.int32),
            pltpu.VMEM((NPAS, 8, HD), jnp.float32),
            pltpu.VMEM(queries.shape, bf16),
            pltpu.VMEM(question_kv.shape, bf16),
            pltpu.VMEM((2, KEYS, HD), bf16),
            pltpu.VMEM((R_DEV, 2, KEYS, HD), bf16),
            pltpu.VMEM((R_DEV, 2, GROUPS * QLEN, KEYS), bf16),
            pltpu.VMEM((R_DEV, QLEN, QH // HEADS * HD), bf16),
            dma((CHUNKS,)), dma((CHUNKS,)),
            dma((CHUNKS, 7)), dma((CHUNKS, 7)),
            dma((CHUNKS, ZS)), dma((CHUNKS, ZS)),
            dma((ZS,)), dma((ZS,)),
            dma((HEADS + 4,)), dma((R_DEV,)),
        ],
        compiler_params=pltpu.CompilerParams(
            collective_id=0, has_side_effects=True, vmem_limit_bytes=48 * 1024 * 1024
        ),
    )(passage_ids, rows, scales, queries, question_kv, jnp.asarray(rope_table()))


def per_device(queries, question_kv, pages, page_scales, passage_ids):
    args = (queries, question_kv, pages, page_scales, passage_ids)
    result, flags = fast(*args)
    return lax.cond(flags[0, HD - 1] > 0, lambda: general(*args), lambda: result)


def solution(mesh):
    return jax.shard_map(
        per_device,
        mesh=mesh,
        in_specs=(
            P("store", "head"),
            P("store", "head"),
            P("store", "head", None),
            P("store", "head", None),
            P("store", None),
        ),
        out_specs=P("store", "head"),
        check_vma=False,
    )
```

time: 126 us -> 110 us (0.87)
  Pallas kernels: 120 us -> 105 us
  local copies, waits for them, and re-layouts: 5.28 us -> 3.64 us
    pallas_call x1, Pallas kernels: 120 us -> 105 us  [fast(): pl.pallas_call(kernel, out_shape=(jax.ShapeDtypeStruct(queries.shape, bf1...]
    unnamed x16 -> x13, local copies, waits for them, and re-layouts: 4.76 us -> 3.05 us
where the time goes in v2:
time: 110 us; the launch traced here: 109 us
  Pallas kernels  105 us (95%)
  local copies, waits for them, and re-layouts  3.64 us (3%)
    pallas_call x1, Pallas kernels, fast(): pl.pallas_call(kernel, out_shape=(jax.ShapeDtypeStruct(queries.shape, bf1...  105 us
    unnamed x13, local copies, waits for them, and re-layouts  3.05 us

profile of v2, /device:TPU:1, one launch (start us, length us, event | category | flops | bytes accessed | tf_op | source)
XLA Modules:
  0.0 109.1 jit_solution(15350095365354807810)
XLA Ops:
  0.0 0.0 copy-start.6
  0.0 0.0 copy-start
  0.0 0.7 copy-done
  0.7 0.0 copy-start.1
  0.7 0.0 copy-start.2
  0.7 0.0 copy-start.3
  0.7 0.0 copy-start.4
  0.7 104.5 %shard_map.66 = (bf16[256,2048]{1,0:T(8,128)(2,1)}, f32[8,128]{1,0:T(8,128)S(1)}) custom-call(s32[4,4]{1,0:T(4,128)} %ids_ref.1, bf16[384,2048]{1,0:T(8,128)(2,1)} %bitcast.100, bf16[256,24]{1,0:T(8,128)(2,1)} %bitcast.107, bf16[256,2048]{1,0:T(8,128)(2,1)} %q_ref.1, bf16[256,512]{1,0:T(8,128)(2,1)} %qkv_ref.1, f32[4,8,128]{2,1,0:T(8,128)S(1)} %copy-done), custom_call_target="tpu_custom_call" | custom-call | tf_op jit(solution)/shard_map/pallas_call | solution.py:514
  105.3 0.6 slice.22
  106.5 0.0 copy-done.6
  106.5 0.0 copy-done.1
  106.5 0.0 copy-done.2
  106.6 0.0 copy-done.3
  106.6 0.0 copy-done.4
  106.6 0.2 conditional.1
  106.8 2.3 %copy.152 = bf16[256,2048]{1,0:T(8,128)(2,1)} copy(bf16[256,2048]{1,0:T(8,128)(2,1)} %get-tuple-element.55) | data formatting | bytes 2097152
Async XLA Ops:
  0.0 106.5 %copy-start.6 = (s32[4,4]{1,0:T(4,128)S(1)}, s32[4,4]{1,0:T(4,128)}, u32[]{:S(2)}) copy-start(s32[4,4]{1,0:T(4,128)} %ids_ref.1) | copy-start | bytes 196
  0.0 0.7 copy-start
  0.7 105.8 %copy-start.1 = (bf16[16,24,2048]{2,1,0:T(8,128)(2,1)S(1)}, bf16[16,24,2048]{2,1,0:T(8,128)(2,1)}, u32[]{:S(2)}) copy-start(bf16[16,24,2048]{2,1,0:T(8,128)(2,1)} %param.12) | copy-start | bytes 4718596
  0.7 105.8 %copy-start.2 = (bf16[16,24,16]{1,2,0:T(8,128)(2,1)S(1)}, bf16[16,24,16]{1,2,0:T(8,128)(2,1)}, u32[]{:S(2)}) copy-start(bf16[16,24,16]{1,2,0:T(8,128)(2,1)} %param.13) | copy-start | bytes 36868
  0.7 105.8 %copy-start.3 = (bf16[256,2048]{1,0:T(8,128)(2,1)S(1)}, bf16[256,2048]{1,0:T(8,128)(2,1)}, u32[]{:S(2)}) copy-start(bf16[256,2048]{1,0:T(8,128)(2,1)} %q_ref.1) | copy-start | bytes 3145732
  0.7 105.8 %copy-start.4 = (bf16[256,512]{1,0:T(8,128)(2,1)S(1)}, bf16[256,512]{1,0:T(8,128)(2,1)}, u32[]{:S(2)}) copy-start(bf16[256,512]{1,0:T(8,128)(2,1)} %qkv_ref.1) | copy-start | bytes 786436

commit v3 on v2

--- a/solution.py
+++ b/solution.py
@@ -29,10 +29,22 @@
 PIECE = NPAS * TOK
 PKEYS = NPAS * PLEN
 KEYS = PKEYS + QLEN
-CHUNKS = 2 * HEADS
+CHUNKS = 2 * HEADS + 1
+REST = CHUNKS - 1
+FIRST = 16
+ORDER = (0, REST, 4, 1, 3, 2, 5, 7, 6)
+LAST = ORDER[-1] - HEADS
 MESH = pl.DeviceIdType.MESH
 
 rope_theta = 500000.0
+
+
+def rows_of(n):
+    return FIRST if n == 0 else ROWS - FIRST if n == REST else ROWS
+
+
+def holds_keys(n):
+    return n < HEADS or n == REST
 
 
 def rotate_keys(keys, offsets):
@@ -161,16 +173,17 @@
 def kernel(
     ids_ref, pages_ref, scales_ref, q_ref, qkv_ref, rope_ref,
     out_ref, flag_ref,
-    p0, p1, p2, p3, yk1, yk2, yk3, yv1, yv2, yv3, gk0, gk1, gk2, gk3, gv0, gv1, gv2, gv3,
-    s0, s1, s2, s3, s4, s5, s6, s7, l0, l1, l2, l3, l4, l5, l6, l7,
-    idv, ids, want, mine, rope, queries, question, keys, values, probs, result,
+    p0, p1, p2, p3, yk1, yk2, yk3, yv1, yv2, yv3, gk0, gk1, gk2, gk3, gv0, gv1, gv2, gv3, gk4,
+    s0, s1, s2, s3, s4, s5, s6, s7, s8, l0, l1, l2, l3, l4, l5, l6, l7, l8,
+    idv, ids, mine, rope, scaling, queries, question, keys, values, late, probs, late_probs, sums,
+    result,
     y_send, y_recv, x_send, x_recv, z_send, z_recv, i_send, i_recv, in_sem, out_sem,
 ):
     parts = (p0, p1, p2, p3)
-    outward = (None, yk1, yk2, yk3, None, yv1, yv2, yv3)
-    gathered = (gk0, gk1, gk2, gk3, gv0, gv1, gv2, gv3)
-    outgoing = (s0, s1, s2, s3, s4, s5, s6, s7)
-    landed = (l0, l1, l2, l3, l4, l5, l6, l7)
+    outward = (None, yk1, yk2, yk3, None, yv1, yv2, yv3, None)
+    gathered = (gk0, gk1, gk2, gk3, gv0, gv1, gv2, gv3, gk4)
+    outgoing = (s0, s1, s2, s3, s4, s5, s6, s7, s8)
+    landed = (l0, l1, l2, l3, l4, l5, l6, l7, l8)
     store, head = lax.axis_index("store"), lax.axis_index("head")
     x, z, core = store // (ZS * CORES), (store // CORES) % ZS, store % CORES
     turn = 1 - 2 * core
@@ -195,6 +208,8 @@
         lanes = pl.ds(pl.multiple_of(to * PART, PART), PART)
         return pltpu.make_async_copy(pages_ref.at[:, lanes], parts[c], in_sem.at[c])
 
+    scale_copy = pltpu.make_async_copy(scales_ref, scaling, in_sem.at[HEADS + 4])
+    scale_copy.start()
     for c in range(HEADS):
         page_copy(c).start()
     rope_copy = pltpu.make_async_copy(rope_ref, rope, in_sem.at[HEADS])
@@ -205,6 +220,9 @@
     question_copy.start()
 
     planes, over = [], 0
+    lane8 = lax.broadcasted_iota(jnp.int32, (8, 128), 1)
+    row8 = lax.broadcasted_iota(jnp.int32, (8, 128), 0)
+    tile = jnp.zeros((8, 128), jnp.int32)
     for i in range(FETCH):
         one = ids_ref[i // NPAS, i % NPAS]
         plane = (one // P_DEV // CORES) % ZS
@@ -214,11 +232,9 @@
         planes.append(plane)
         over = jnp.maximum(over, rank)
         mine[i] = plane * SLOTS + jnp.minimum(rank, SLOTS - 1)
-    lane8 = lax.broadcasted_iota(jnp.int32, (8, 128), 1)
-    tile = jnp.where(lane8 == FETCH, over, 0)
-    for i in range(FETCH):
-        tile = jnp.where(lane8 == i, ids_ref[i // NPAS, i % NPAS], tile)
-    idv[z] = tile
+        code = one + (i % NPAS) * (XS * ZS * CORES * P_DEV)
+        tile = jnp.where((lane8 == rank) & (row8 == plane), code, tile)
+    idv[z] = jnp.where(lane8 == FETCH, over, tile)
 
     def id_copy(step):
         return pltpu.make_async_remote_copy(
@@ -266,13 +282,27 @@
     def scales_of(col):
         pick = jnp.where(pick_row == 2 * KVH * pick_lane + col, 1.0, 0.0).astype(jnp.bfloat16)
         return lax.dot_general(
-            scales_ref[...], pick, (((0,), (0,)), ((), ())), preferred_element_type=jnp.float32
+            scaling[...], pick, (((0,), (0,)), ((), ())), preferred_element_type=jnp.float32
         )
 
-    def lay_out(c, key_blocks, value_blocks, *at_):
+    def lay_out(c):
         first = 4 * ((head + HEADS - c) % HEADS)
         scales = [scales_of(first + j) for j in range(4)]
-        key_blocks[(*at_, P_DEV)] = jnp.concatenate([scales[0], scales[2]], axis=0).astype(jnp.bfloat16)
+
+        def put_keys(p, rows):
+            if c == 0:
+                gk0[here, p] = rows[:FIRST].astype(jnp.bfloat16)
+                gk4[here, p] = rows[FIRST:].astype(jnp.bfloat16)
+            else:
+                outward[c][p] = rows.astype(jnp.bfloat16)
+
+        def put_values(p, rows):
+            if c == 0:
+                gv0[here, p] = rows.astype(jnp.bfloat16)
+            else:
+                outward[HEADS + c][p] = rows.astype(jnp.bfloat16)
+
+        put_keys(P_DEV, jnp.concatenate([scales[0], scales[2]], axis=0))
 
         def two_pages(i, carry):
             pair = pl.ds(pl.multiple_of(i * ROWS, ROWS), ROWS)
@@ -287,9 +317,8 @@
                         jnp.where(lane == p, scales[2 * g + 1], 0.0), axis=1, keepdims=True
                     )
                     value_half.append(codes[g][rows, HD:] * scale)
-                key_half = [codes[g][rows, :HD] for g in range(2)]
-                key_blocks[(*at_, p)] = jnp.concatenate(key_half, axis=0).astype(jnp.bfloat16)
-                value_blocks[(*at_, p)] = jnp.concatenate(value_half, axis=0).astype(jnp.bfloat16)
+                put_keys(p, jnp.concatenate([codes[g][rows, :HD] for g in range(2)], axis=0))
+                put_values(p, jnp.concatenate(value_half, axis=0))
             return carry
 
         lax.fori_loop(0, P_DEV // 2, two_pages, 0)
@@ -318,16 +347,15 @@
         for kind in (3, 4, 5, 6):
             x_copy(n, kind).wait_recv()
 
-    rows_lane = lax.broadcasted_iota(jnp.int32, (ROWS, 128), 1)
-
     def finished(n, code):
         slot = code % P_DEV
         shard = (code // P_DEV) % (XS * ZS * CORES)
         k = code // (XS * ZS * CORES * P_DEV)
         place = (shard // (ZS * CORES)) * CORES + shard % CORES
         block = gathered[n][place, slot]
-        if n >= HEADS:
+        if not holds_keys(n):
             return block
+        rows_lane = lax.broadcasted_iota(jnp.int32, (rows_of(n), 128), 1)
         scales = gathered[n][place, P_DEV].astype(jnp.float32)
         scale = jnp.sum(jnp.where(rows_lane == slot, scales, 0.0), axis=1, keepdims=True)
         key = block.astype(jnp.float32) * scale
@@ -339,26 +367,26 @@
             step = (i * 3) % ZS
             to = (z + step) % ZS
             for j in range(SLOTS):
-                outgoing[n][step, j] = finished(n, want[to * SLOTS + j])
+                outgoing[n][step, j] = finished(n, ids[to, z, j])
             z_copy(n, step).start()
             return carry
 
         lax.fori_loop(1, ZS, one_dest, 0)
         for j in range(SLOTS):
-            landed[n][z, j] = finished(n, want[z * SLOTS + j])
-
+            landed[n][z, j] = finished(n, ids[z, z, j])
+
+    scale_copy.wait()
     page_copy(0).wait()
-    lay_out(0, gk0, gv0, here)
+    lay_out(0)
     pl.semaphore_wait(barrier, len(peers))
     for step in range(1, ZS):
         id_copy(step).start()
-    x_start(0)
-    for c in range(1, HEADS):
+    x_start(ORDER[0])
+    x_start(ORDER[1])
+    for c in (1, 3, 2):
         page_copy(c).wait()
-        lay_out(c, outward[c], outward[HEADS + c])
+        lay_out(c)
         y_copy(c).start()
-    for c in range(1, HEADS):
-        y_copy(HEADS + c).start()
     rope_copy.wait()
 
     for step in range(1, ZS):
@@ -367,33 +395,28 @@
     to_smem.start()
     to_smem.wait()
 
-    def scan(dest, worst):
-        count = 0
-        chosen = [0] * SLOTS
-        for i in range(FETCH):
-            one = ids[dest, 0, i]
-            hit = (one // P_DEV // CORES) % ZS == z
-            for j in range(SLOTS):
-                chosen[j] = jnp.where(
-                    hit & (count == j), one + (i % NPAS) * (XS * ZS * CORES * P_DEV), chosen[j]
-                )
-            count = count + jnp.where(hit, 1, 0)
-        for j in range(SLOTS):
-            want[dest * SLOTS + j] = chosen[j]
-        return jnp.maximum(worst, ids[dest, 0, FETCH])
-
     x_forward(0)
-    worst = lax.fori_loop(0, ZS, scan, jnp.int32(0))
+    worst = ids[0, 0, FETCH]
+    for dest in range(1, ZS):
+        worst = jnp.maximum(worst, ids[dest, 0, FETCH])
     flag = jnp.where(worst >= SLOTS, 1.0, 0.0)
 
-    for n in range(CHUNKS):
-        if n > 0:
-            x_forward(n)
-        if n + 1 < CHUNKS:
-            x_start(n + 1)
-        x_last(n)
-        x_done(n)
-        z_start(n)
+    x_start(ORDER[2])
+    x_last(0)
+    x_forward(ORDER[1])
+    x_done(0)
+    z_start(0)
+    x_start(ORDER[3])
+    for n in ORDER[6:]:
+        y_copy(n).start()
+    for i in range(1, CHUNKS):
+        x_last(ORDER[i])
+        if i + 1 < CHUNKS:
+            x_forward(ORDER[i + 1])
+        if i + 3 < CHUNKS:
+            x_start(ORDER[i + 3])
+        x_done(ORDER[i])
+        z_start(ORDER[i])
 
     flags = gk3[0, P_DEV].astype(jnp.float32)
     for place in range(1, SHARDS):
@@ -407,11 +430,12 @@
 
         lax.fori_loop(1, ZS, one, 0)
 
-    def passages(n, r):
+    def passages(ns, r):
         blocks = []
         for k in range(NPAS):
             place = mine[r * NPAS + k]
-            blocks.append(landed[n][place // SLOTS, place % SLOTS].astype(jnp.float32))
+            pieces = [landed[n][place // SLOTS, place % SLOTS].astype(jnp.float32) for n in ns]
+            blocks.append(pieces[0] if len(ns) == 1 else jnp.concatenate(pieces, axis=0))
         return [
             jnp.concatenate([b[g * TOK : (g + 1) * TOK] for b in blocks], axis=0).astype(
                 jnp.bfloat16
@@ -419,8 +443,9 @@
             for g in range(2)
         ]
 
-    for c in range(HEADS):
-        arrived(c)
+    early = [c for c in (0, 1, 3, 2) if c != LAST]
+    for n in [n for n in ORDER if holds_keys(n)]:
+        arrived(n)
     query_copy.wait()
     question_copy.wait()
 
@@ -430,12 +455,12 @@
 
     def weigh(r, carry):
         rows = pl.ds(pl.multiple_of(r * QLEN, QLEN), QLEN)
-        for c in range(HEADS):
-            for g, part in enumerate(passages(c, r)):
-                keys[g, c * PIECE : (c + 1) * PIECE, :] = part
+        for i, c in enumerate(early + [LAST]):
+            for g, part in enumerate(passages((0, REST) if c == 0 else (c,), r)):
+                keys[g, i * PIECE : (i + 1) * PIECE, :] = part
         for g in range(2):
             keys[g, PKEYS:, :] = question[rows, g * LANES : g * LANES + HD]
-            values[r, g, PKEYS:, :] = question[rows, g * LANES + HD : (g + 1) * LANES]
+            values[r, g, PKEYS - PIECE :, :] = question[rows, g * LANES + HD : (g + 1) * LANES]
             query = jnp.concatenate(
                 [
                     queries[rows, (g * GROUPS + j) * HD : (g * GROUPS + j + 1) * HD]
@@ -459,29 +484,43 @@
             now = jnp.exp(now - top)
             total = jnp.sum(past, axis=1, keepdims=True) + jnp.sum(now, axis=1, keepdims=True)
             inverse = 1.0 / total
-            probs[r, g, :, :PKEYS] = (past * inverse).astype(jnp.bfloat16)
-            probs[r, g, :, PKEYS:] = (now * inverse).astype(jnp.bfloat16)
+            past = (past * inverse).astype(jnp.bfloat16)
+            probs[r, g, :, : PKEYS - PIECE] = past[:, : PKEYS - PIECE]
+            probs[r, g, :, PKEYS - PIECE :] = (now * inverse).astype(jnp.bfloat16)
+            late_probs[r, g] = past[:, PKEYS - PIECE :]
         return carry
 
     lax.fori_loop(0, R_DEV, weigh, 0)
 
-    for c in range(HEADS):
+    for i, c in enumerate(early):
         arrived(HEADS + c)
 
-        def place_values(r, carry, c=c):
-            for g, part in enumerate(passages(HEADS + c, r)):
-                values[r, g, c * PIECE : (c + 1) * PIECE, :] = part
+        def place_values(r, carry, i=i, c=c):
+            for g, part in enumerate(passages((HEADS + c,), r)):
+                values[r, g, i * PIECE : (i + 1) * PIECE, :] = part
             return carry
 
         lax.fori_loop(0, R_DEV, place_values, 0)
+
+    def mix_early(r, carry):
+        for g in range(2):
+            sums[r, g] = jnp.dot(probs[r, g], values[r, g], preferred_element_type=jnp.float32)
+        return carry
+
+    lax.fori_loop(0, R_DEV, mix_early, 0)
+    arrived(HEADS + LAST)
 
     def out_copy(r):
         rows = pl.ds(pl.multiple_of(r * QLEN, QLEN), QLEN)
         return pltpu.make_async_copy(result.at[r], out_ref.at[rows], out_sem.at[r])
 
     def mix(r, carry):
+        for g, part in enumerate(passages((HEADS + LAST,), r)):
+            late[g] = part
         for g in range(2):
-            mixed = jnp.dot(probs[r, g], values[r, g], preferred_element_type=jnp.float32)
+            mixed = sums[r, g] + jnp.dot(
+                late_probs[r, g], late[g], preferred_element_type=jnp.float32
+            )
             for j in range(GROUPS):
                 result[r, :, (g * GROUPS + j) * HD : (g * GROUPS + j + 1) * HD] = mixed[
                     j * QLEN : (j + 1) * QLEN
@@ -517,34 +556,39 @@
             jax.ShapeDtypeStruct(queries.shape, bf16),
             jax.ShapeDtypeStruct((8, 128), jnp.float32),
         ),
-        in_specs=[pl.BlockSpec(memory_space=pltpu.SMEM), hbm, vmem, hbm, hbm, hbm],
+        in_specs=[pl.BlockSpec(memory_space=pltpu.SMEM)] + [hbm] * 5,
         out_specs=(hbm, vmem),
         scratch_shapes=[pltpu.VMEM((P_DEV * TOK, PART), bf16)] * HEADS
         + [pltpu.VMEM((P_DEV + 1,) + block, bf16)] * (HEADS - 1)
         + [pltpu.VMEM((P_DEV,) + block, bf16)] * (HEADS - 1)
-        + [pltpu.VMEM((SHARDS, P_DEV + 1) + block, bf16)] * HEADS
-        + [pltpu.VMEM((SHARDS, P_DEV) + block, bf16)] * HEADS
-        + [pltpu.VMEM((ZS, SLOTS) + block, bf16)] * (2 * CHUNKS)
+        + [
+            pltpu.VMEM((SHARDS, P_DEV + holds_keys(n), rows_of(n), HD), bf16)
+            for n in range(CHUNKS)
+        ]
+        + [pltpu.VMEM((ZS, SLOTS, rows_of(n), HD), bf16) for n in range(CHUNKS)] * 2
         + [
             pltpu.VMEM((ZS, 8, 128), jnp.int32),
             pltpu.SMEM((ZS, 8, 128), jnp.int32),
-            pltpu.SMEM((ZS * SLOTS,), jnp.int32),
             pltpu.SMEM((FETCH,), jnp.int32),
             pltpu.VMEM((NPAS, 8, HD), jnp.float32),
+            pltpu.VMEM(scales.shape, bf16),
             pltpu.VMEM(queries.shape, bf16),
             pltpu.VMEM(question_kv.shape, bf16),
             pltpu.VMEM((2, KEYS, HD), bf16),
-            pltpu.VMEM((R_DEV, 2, KEYS, HD), bf16),
-            pltpu.VMEM((R_DEV, 2, GROUPS * QLEN, KEYS), bf16),
+            pltpu.VMEM((R_DEV, 2, KEYS - PIECE, HD), bf16),
+            pltpu.VMEM((2, PIECE, HD), bf16),
+            pltpu.VMEM((R_DEV, 2, GROUPS * QLEN, KEYS - PIECE), bf16),
+            pltpu.VMEM((R_DEV, 2, GROUPS * QLEN, PIECE), bf16),
+            pltpu.VMEM((R_DEV, 2, GROUPS * QLEN, HD), jnp.float32),
             pltpu.VMEM((R_DEV, QLEN, QH // HEADS * HD), bf16),
             dma((CHUNKS,)), dma((CHUNKS,)),
             dma((CHUNKS, 7)), dma((CHUNKS, 7)),
             dma((CHUNKS, ZS)), dma((CHUNKS, ZS)),
             dma((ZS,)), dma((ZS,)),
-            dma((HEADS + 4,)), dma((R_DEV,)),
+            dma((HEADS + 5,)), dma((R_DEV,)),
         ],
         compiler_params=pltpu.CompilerParams(
-            collective_id=0, has_side_effects=True, vmem_limit_bytes=48 * 1024 * 1024
+            collective_id=0, has_side_effects=True, vmem_limit_bytes=58 * 1024 * 1024
         ),
     )(passage_ids, rows, scales, queries, question_kv, jnp.asarray(rope_table()))
 
@@ -552,7 +596,8 @@
 def per_device(queries, question_kv, pages, page_scales, passage_ids):
     args = (queries, question_kv, pages, page_scales, passage_ids)
     result, flags = fast(*args)
-    return lax.cond(flags[0, HD - 1] > 0, lambda: general(*args), lambda: result)
+    full = flags[0, HD - 1] > 0
+    return lax.cond(full, lambda: general(*args), lambda: result)
 
 
 def solution(mesh):

time: 110 us -> 105 us (0.955)
  Pallas kernels: 105 us -> 100 us
    pallas_call x1, Pallas kernels: 105 us -> 100 us  [fast(): pl.pallas_call(kernel, out_shape=(jax.ShapeDtypeStruct(queries.shape, bf1...]
    unnamed x13 -> x11, local copies, waits for them, and re-layouts: 3.05 us -> 2.32 us
where the time goes in v3:
time: 105 us
  Pallas kernels  100 us (95%)
  local copies, waits for them, and re-layouts  3.58 us (3%)
    pallas_call x1, Pallas kernels, fast(): pl.pallas_call(kernel, out_shape=(jax.ShapeDtypeStruct(queries.shape, bf1...  100 us
    unnamed x11, local copies, waits for them, and re-layouts  2.32 us

profile of v3, /device:TPU:1, one launch (start us, length us, event | category | flops | bytes accessed | tf_op | source)
XLA Modules:
  0.0 104.7 jit_solution(2754696337384837376)
XLA Ops:
  0.0 0.0 copy-start.5
  0.0 0.0 copy-start
  0.0 0.0 copy-start.1
  0.0 0.0 copy-start.2
  0.0 0.0 copy-start.3
  0.0 100.2 %shard_map.66 = (bf16[256,2048]{1,0:T(8,128)(2,1)}, f32[8,128]{1,0:T(8,128)}) custom-call(s32[4,4]{1,0:T(4,128)} %ids_ref.1, bf16[384,2048]{1,0:T(8,128)(2,1)} %bitcast.100, bf16[256,24]{1,0:T(8,128)(2,1)} %bitcast.107, bf16[256,2048]{1,0:T(8,128)(2,1)} %q_ref.1, bf16[256,512]{1,0:T(8,128)(2,1)} %qkv_ref.1, f32[4,8,128]{2,1,0:T(8,128)} %constant.114.clone.rope_ref), custom_call_target="tpu_custom_call" | custom-call | tf_op jit(solution)/shard_map/pallas_call | solution.py:553
  100.2 1.3 %slice.22 = f32[1,1]{1,0:T(1,128)} slice(f32[8,128]{1,0:T(8,128)} %get-tuple-element.53), slice={[0:1], [127:128]} | slice | bytes 8 | tf_op jit(solution)/shard_map/slice | solution.py:599
  102.1 0.0 copy-done.5
  102.1 0.0 copy-done
  102.1 0.0 copy-done.1
  102.1 0.0 copy-done.2
  102.2 0.0 copy-done.3
  102.2 0.2 conditional.1
  102.4 2.3 %copy.152 = bf16[256,2048]{1,0:T(8,128)(2,1)} copy(bf16[256,2048]{1,0:T(8,128)(2,1)} %get-tuple-element.55) | data formatting | bytes 2097152
Async XLA Ops:
  0.0 102.1 %copy-start.5 = (s32[4,4]{1,0:T(4,128)S(1)}, s32[4,4]{1,0:T(4,128)}, u32[]{:S(2)}) copy-start(s32[4,4]{1,0:T(4,128)} %ids_ref.1) | copy-start | bytes 196
  0.0 102.1 %copy-start = (bf16[16,24,2048]{2,1,0:T(8,128)(2,1)S(1)}, bf16[16,24,2048]{2,1,0:T(8,128)(2,1)}, u32[]{:S(2)}) copy-start(bf16[16,24,2048]{2,1,0:T(8,128)(2,1)} %param.12) | copy-start | bytes 4718596
  0.0 102.1 %copy-start.1 = (bf16[16,24,16]{1,2,0:T(8,128)(2,1)S(1)}, bf16[16,24,16]{1,2,0:T(8,128)(2,1)}, u32[]{:S(2)}) copy-start(bf16[16,24,16]{1,2,0:T(8,128)(2,1)} %param.13) | copy-start | bytes 36868
  0.0 102.1 %copy-start.2 = (bf16[256,2048]{1,0:T(8,128)(2,1)S(1)}, bf16[256,2048]{1,0:T(8,128)(2,1)}, u32[]{:S(2)}) copy-start(bf16[256,2048]{1,0:T(8,128)(2,1)} %q_ref.1) | copy-start | bytes 3145732
  0.0 102.1 %copy-start.3 = (bf16[256,512]{1,0:T(8,128)(2,1)S(1)}, bf16[256,512]{1,0:T(8,128)(2,1)}, u32[]{:S(2)}) copy-start(bf16[256,512]{1,0:T(8,128)(2,1)} %qkv_ref.1) | copy-start | bytes 786436

commit v4 on v3

--- a/solution.py
+++ b/solution.py
@@ -383,10 +383,14 @@
         id_copy(step).start()
     x_start(ORDER[0])
     x_start(ORDER[1])
-    for c in (1, 3, 2):
+    for c in (1, 3):
         page_copy(c).wait()
         lay_out(c)
         y_copy(c).start()
+    x_forward(ORDER[0])
+    page_copy(2).wait()
+    lay_out(2)
+    y_copy(2).start()
     rope_copy.wait()
 
     for step in range(1, ZS):
@@ -395,7 +399,6 @@
     to_smem.start()
     to_smem.wait()
 
-    x_forward(0)
     worst = ids[0, 0, FETCH]
     for dest in range(1, ZS):
         worst = jnp.maximum(worst, ids[dest, 0, FETCH])
@@ -406,22 +409,21 @@
     x_forward(ORDER[1])
     x_done(0)
     z_start(0)
-    x_start(ORDER[3])
     for n in ORDER[6:]:
         y_copy(n).start()
     for i in range(1, CHUNKS):
         x_last(ORDER[i])
         if i + 1 < CHUNKS:
             x_forward(ORDER[i + 1])
-        if i + 3 < CHUNKS:
-            x_start(ORDER[i + 3])
+        if i + 2 < CHUNKS:
+            x_start(ORDER[i + 2])
         x_done(ORDER[i])
         z_start(ORDER[i])
 
     flags = gk3[0, P_DEV].astype(jnp.float32)
     for place in range(1, SHARDS):
         flags = jnp.maximum(flags, gk3[place, P_DEV].astype(jnp.float32))
-    flag_ref[...] = flags[:8]
+    flag_ref[0, 0] = jnp.max(flags[:8, HD // 2 :]).astype(jnp.int32)
 
     def arrived(n):
         def one(step, carry):
@@ -544,7 +546,7 @@
 
 
 def fast(queries, question_kv, pages, page_scales, passage_ids):
-    vmem = pl.BlockSpec(memory_space=pltpu.VMEM)
+    smem = pl.BlockSpec(memory_space=pltpu.SMEM)
     hbm = pl.BlockSpec(memory_space=pl.ANY)
     block = (ROWS, HD)
     dma, bf16 = pltpu.SemaphoreType.DMA, jnp.bfloat16
@@ -554,10 +556,10 @@
         kernel,
         out_shape=(
             jax.ShapeDtypeStruct(queries.shape, bf16),
-            jax.ShapeDtypeStruct((8, 128), jnp.float32),
+            jax.ShapeDtypeStruct((1, 1), jnp.int32),
         ),
-        in_specs=[pl.BlockSpec(memory_space=pltpu.SMEM)] + [hbm] * 5,
-        out_specs=(hbm, vmem),
+        in_specs=[smem] + [hbm] * 5,
+        out_specs=(hbm, smem),
         scratch_shapes=[pltpu.VMEM((P_DEV * TOK, PART), bf16)] * HEADS
         + [pltpu.VMEM((P_DEV + 1,) + block, bf16)] * (HEADS - 1)
         + [pltpu.VMEM((P_DEV,) + block, bf16)] * (HEADS - 1)
@@ -595,8 +597,8 @@
 
 def per_device(queries, question_kv, pages, page_scales, passage_ids):
     args = (queries, question_kv, pages, page_scales, passage_ids)
-    result, flags = fast(*args)
-    full = flags[0, HD - 1] > 0
+    result, flag = fast(*args)
+    full = flag[0, 0] > 0
     return lax.cond(full, lambda: general(*args), lambda: result)
 
 

time: 105 us -> 102 us (0.971)
  Pallas kernels: 100 us -> 97.8 us
  local copies, waits for them, and re-layouts: 3.58 us -> 2.32 us
    pallas_call x1, Pallas kernels: 100 us -> 97.8 us  [fast(): pl.pallas_call(kernel, out_shape=(jax.ShapeDtypeStruct(queries.shape, bf1...]
    slice x1 -> x0, local copies, waits for them, and re-layouts: 1.26 us -> none  [per_device(): full = flags[0, HD - 1] > 0]
where the time goes in v4:
time: 102 us; the launch traced here: 101 us
  Pallas kernels  97.8 us (96%)
  local copies, waits for them, and re-layouts  2.32 us (2%)
    pallas_call x1, Pallas kernels, fast(): pl.pallas_call(kernel, out_shape=(jax.ShapeDtypeStruct(queries.shape, bf1...  97.8 us
    unnamed x11, local copies, waits for them, and re-layouts  2.32 us

profile of v4, /device:TPU:1, one launch (start us, length us, event | category | flops | bytes accessed | tf_op | source)
XLA Modules:
  0.0 101.0 jit_solution(4995250409352219649)
XLA Ops:
  0.0 0.0 copy-start.5
  0.0 0.0 copy-start
  0.0 0.0 copy-start.1
  0.0 0.0 copy-start.2
  0.0 0.0 copy-start.3
  0.0 97.8 %shard_map.66 = (bf16[256,2048]{1,0:T(8,128)(2,1)}, s32[1,1]{1,0:T(1,128)}) custom-call(s32[4,4]{1,0:T(4,128)} %ids_ref.1, bf16[384,2048]{1,0:T(8,128)(2,1)} %bitcast.100, bf16[256,24]{1,0:T(8,128)(2,1)} %bitcast.107, bf16[256,2048]{1,0:T(8,128)(2,1)} %q_ref.1, bf16[256,512]{1,0:T(8,128)(2,1)} %qkv_ref.1, f32[4,8,128]{2,1,0:T(8,128)} %constant.114.clone.rope_ref), custom_call_target="tpu_custom_call" | custom-call | tf_op jit(solution)/shard_map/pallas_call | solution.py:555
  98.4 0.0 copy-done.5
  98.4 0.0 copy-done
  98.4 0.0 copy-done.1
  98.4 0.0 copy-done.2
  98.5 0.0 copy-done.3
  98.5 0.2 conditional.1
  98.7 2.3 %copy.152 = bf16[256,2048]{1,0:T(8,128)(2,1)} copy(bf16[256,2048]{1,0:T(8,128)(2,1)} %get-tuple-element.55) | data formatting | bytes 2097152
Async XLA Ops:
  0.0 98.4 %copy-start.5 = (s32[4,4]{1,0:T(4,128)S(1)}, s32[4,4]{1,0:T(4,128)}, u32[]{:S(2)}) copy-start(s32[4,4]{1,0:T(4,128)} %ids_ref.1) | copy-start | bytes 196
  0.0 98.4 %copy-start = (bf16[16,24,2048]{2,1,0:T(8,128)(2,1)S(1)}, bf16[16,24,2048]{2,1,0:T(8,128)(2,1)}, u32[]{:S(2)}) copy-start(bf16[16,24,2048]{2,1,0:T(8,128)(2,1)} %param.12) | copy-start | bytes 4718596
  0.0 98.4 %copy-start.1 = (bf16[16,24,16]{1,2,0:T(8,128)(2,1)S(1)}, bf16[16,24,16]{1,2,0:T(8,128)(2,1)}, u32[]{:S(2)}) copy-start(bf16[16,24,16]{1,2,0:T(8,128)(2,1)} %param.13) | copy-start | bytes 36868
  0.0 98.4 %copy-start.2 = (bf16[256,2048]{1,0:T(8,128)(2,1)S(1)}, bf16[256,2048]{1,0:T(8,128)(2,1)}, u32[]{:S(2)}) copy-start(bf16[256,2048]{1,0:T(8,128)(2,1)} %q_ref.1) | copy-start | bytes 3145732
  0.0 98.4 %copy-start.3 = (bf16[256,512]{1,0:T(8,128)(2,1)S(1)}, bf16[256,512]{1,0:T(8,128)(2,1)}, u32[]{:S(2)}) copy-start(bf16[256,512]{1,0:T(8,128)(2,1)} %qkv_ref.1) | copy-start | bytes 786436

commit v5 on v4

--- a/solution.py
+++ b/solution.py
@@ -252,7 +252,13 @@
             device_id=(store, to), device_id_type=MESH,
         )
 
-    def x_copy(n, kind):
+    def pieces(n):
+        blocks = P_DEV + holds_keys(n)
+        if n in (0, REST):
+            return ((n, pl.ds(0, blocks)),)
+        return (n, pl.ds(0, P_DEV // 2)), (CHUNKS + n, pl.ds(P_DEV // 2, blocks - P_DEV // 2))
+
+    def x_copy(n, kind, piece):
         slot, to = (
             (here, at(x + 1, z, core)),
             (here, at(x - 1, z, core)),
@@ -263,8 +269,8 @@
             (spot(x + 2, core), at(x, z, 1 - core)),
         )[kind]
         return pltpu.make_async_remote_copy(
-            src_ref=gathered[n].at[slot], dst_ref=gathered[n].at[slot],
-            send_sem=x_send.at[n, kind], recv_sem=x_recv.at[n, kind],
+            src_ref=gathered[n].at[slot, piece[1]], dst_ref=gathered[n].at[slot, piece[1]],
+            send_sem=x_send.at[piece[0], kind], recv_sem=x_recv.at[piece[0], kind],
             device_id=(to, head), device_id_type=MESH,
         )
 
@@ -330,22 +336,26 @@
             gk3[here, P_DEV, :, HD // 2 :] = jnp.broadcast_to(flag, (ROWS, HD // 2)).astype(
                 jnp.bfloat16
             )
-        for kind in (0, 1, 3):
-            x_copy(n, kind).start()
+        for piece in pieces(n):
+            for kind in (0, 1, 3):
+                x_copy(n, kind, piece).start()
 
     def x_forward(n):
-        x_copy(n, 0).wait_recv()
-        x_copy(n, 1).wait_recv()
-        for kind in (2, 4, 5):
-            x_copy(n, kind).start()
+        for piece in pieces(n):
+            x_copy(n, 0, piece).wait_recv()
+            x_copy(n, 1, piece).wait_recv()
+            for kind in (2, 4, 5):
+                x_copy(n, kind, piece).start()
 
     def x_last(n):
-        x_copy(n, 2).wait_recv()
-        x_copy(n, 6).start()
+        for piece in pieces(n):
+            x_copy(n, 2, piece).wait_recv()
+            x_copy(n, 6, piece).start()
 
     def x_done(n):
-        for kind in (3, 4, 5, 6):
-            x_copy(n, kind).wait_recv()
+        for piece in pieces(n):
+            for kind in (3, 4, 5, 6):
+                x_copy(n, kind, piece).wait_recv()
 
     def finished(n, code):
         slot = code % P_DEV
@@ -530,15 +540,16 @@
         out_copy(r).start()
         return carry
 
-    lax.fori_loop(0, R_DEV, mix, 0)
+    lax.fori_loop(0, R_DEV, mix, 0, unroll=True)
 
     for step in range(1, ZS):
         id_copy(step).wait_send()
     for n in range(CHUNKS):
         if n % HEADS > 0:
             y_copy(n).wait_send()
-        for kind in range(7):
-            x_copy(n, kind).wait_send()
+        for piece in pieces(n):
+            for kind in range(7):
+                x_copy(n, kind, piece).wait_send()
         for step in range(1, ZS):
             z_copy(n, step).wait_send()
     for r in range(R_DEV):
@@ -584,7 +595,7 @@
             pltpu.VMEM((R_DEV, 2, GROUPS * QLEN, HD), jnp.float32),
             pltpu.VMEM((R_DEV, QLEN, QH // HEADS * HD), bf16),
             dma((CHUNKS,)), dma((CHUNKS,)),
-            dma((CHUNKS, 7)), dma((CHUNKS, 7)),
+            dma((2 * CHUNKS, 7)), dma((2 * CHUNKS, 7)),
             dma((CHUNKS, ZS)), dma((CHUNKS, ZS)),
             dma((ZS,)), dma((ZS,)),
             dma((HEADS + 5,)), dma((R_DEV,)),

time: 102 us -> 101 us (level); the launches traced: 101 us -> 101 us
  no operation moved by 1% of the time
where the time goes in v5:
time: 101 us
  Pallas kernels  98 us (97%)
  local copies, waits for them, and re-layouts  2.32 us (2%)
    pallas_call x1, Pallas kernels, fast(): pl.pallas_call(kernel, out_shape=(jax.ShapeDtypeStruct(queries.shape, bf1...  98 us
    unnamed x11, local copies, waits for them, and re-layouts  2.32 us

profile of v5, /device:TPU:1, one launch (start us, length us, event | category | flops | bytes accessed | tf_op | source)
XLA Modules:
  0.0 101.3 jit_solution(9815786350369864774)
XLA Ops:
  0.0 0.0 copy-start.5
  0.0 0.0 copy-start
  0.0 0.0 copy-start.1
  0.0 0.0 copy-start.2
  0.0 0.0 copy-start.3
  0.0 98.0 %shard_map.66 = (bf16[256,2048]{1,0:T(8,128)(2,1)}, s32[1,1]{1,0:T(1,128)}) custom-call(s32[4,4]{1,0:T(4,128)} %ids_ref.1, bf16[384,2048]{1,0:T(8,128)(2,1)} %bitcast.100, bf16[256,24]{1,0:T(8,128)(2,1)} %bitcast.107, bf16[256,2048]{1,0:T(8,128)(2,1)} %q_ref.1, bf16[256,512]{1,0:T(8,128)(2,1)} %qkv_ref.1, f32[4,8,128]{2,1,0:T(8,128)} %constant.114.clone.rope_ref), custom_call_target="tpu_custom_call" | custom-call | tf_op jit(solution)/shard_map/pallas_call | solution.py:566
  98.7 0.0 copy-done.5
  98.7 0.0 copy-done
  98.7 0.0 copy-done.1
  98.7 0.0 copy-done.2
  98.7 0.0 copy-done.3
  98.7 0.2 conditional.1
  99.0 2.3 %copy.152 = bf16[256,2048]{1,0:T(8,128)(2,1)} copy(bf16[256,2048]{1,0:T(8,128)(2,1)} %get-tuple-element.55) | data formatting | bytes 2097152
Async XLA Ops:
  0.0 98.7 %copy-start.5 = (s32[4,4]{1,0:T(4,128)S(1)}, s32[4,4]{1,0:T(4,128)}, u32[]{:S(2)}) copy-start(s32[4,4]{1,0:T(4,128)} %ids_ref.1) | copy-start | bytes 196
  0.0 98.7 %copy-start = (bf16[16,24,2048]{2,1,0:T(8,128)(2,1)S(1)}, bf16[16,24,2048]{2,1,0:T(8,128)(2,1)}, u32[]{:S(2)}) copy-start(bf16[16,24,2048]{2,1,0:T(8,128)(2,1)} %param.12) | copy-start | bytes 4718596
  0.0 98.7 %copy-start.1 = (bf16[16,24,16]{1,2,0:T(8,128)(2,1)S(1)}, bf16[16,24,16]{1,2,0:T(8,128)(2,1)}, u32[]{:S(2)}) copy-start(bf16[16,24,16]{1,2,0:T(8,128)(2,1)} %param.13) | copy-start | bytes 36868
  0.0 98.7 %copy-start.2 = (bf16[256,2048]{1,0:T(8,128)(2,1)S(1)}, bf16[256,2048]{1,0:T(8,128)(2,1)}, u32[]{:S(2)}) copy-start(bf16[256,2048]{1,0:T(8,128)(2,1)} %q_ref.1) | copy-start | bytes 3145732
  0.0 98.7 %copy-start.3 = (bf16[256,512]{1,0:T(8,128)(2,1)S(1)}, bf16[256,512]{1,0:T(8,128)(2,1)}, u32[]{:S(2)}) copy-start(bf16[256,512]{1,0:T(8,128)(2,1)} %qkv_ref.1) | copy-start | bytes 786436
